TPU v7x, 512 devices: a whole 4x8x8 slice. The times are simulated.
512 devices in a mesh: outer: 16 (over z, y_lo), inner: 32 (over x, y_hi, core).
Axes of the slice: x: 4, y: 8 (y_hi: 4, y_lo: 2; y = y_hi * 2 + y_lo), z: 8, core: 2. Of those that a mesh axis runs over, the one named last changes fastest.
Arguments:
- queries: bfloat16 [131072, 1024], P(('outer', 'inner')), may hold values from -6 to 6
- keys: bfloat16 [131072, 128], P(('outer', 'inner')), may hold values from -6 to 6
- values: bfloat16 [131072, 128], P(('outer', 'inner')), may hold values from -6 to 6
- outputs: bfloat16 [131072, 1024], P(('outer', 'inner')), may hold values from -1.5 to 1.5
- out_grads: bfloat16 [131072, 1024], P(('outer', 'inner')), may hold values from -48 to 48
- log_sum_exp: float32 [8, 131072], P(None, ('outer', 'inner')), may hold values from 5 to 7
- span_ids: int32 [2, 512], replicated, may hold values from 0 to 1023, as said below
Outputs:
- query_grads: float32 [131072, 1024], P(('outer', 'inner'))
- key_grads: float32 [131072, 128], P(('outer', 'inner'))
- value_grads: float32 [131072, 128], P(('outer', 'inner'))
Inputs may be any that keep to these rules, and one draw needn't show every extreme that they name: `span_ids`: column b holds two span numbers c and 1023 - c; each number from 0 to 1023 stands once in the array.
All inputs are finite; a program needn't handle non-finite values.
Results may differ from a plain program's by a relative error of at most 0.0042.
Values may be sent and summed in bfloat16 or wider, within the bound.
A program may use at most 64 MiB of HBM per device.

v0:
```python
import jax
import jax.numpy as jnp
from jax import lax
from jax.sharding import PartitionSpec as P

INNER_STEPS = 4


def passed_along(value, axis, steps):
    count = lax.axis_size(axis)
    pairs = [(source, (source + steps) % count) for source in range(count)]
    return lax.ppermute(value, axis, pairs)


def pair_grads(
    query_heads, grad_heads, log_norm, deltas, key_block, value_block, query_place, key_place
):
    scaling = key_block.shape[1] ** (-0.5)
    scores = (
        jnp.einsum("qhd,kd->hqk", query_heads, key_block, preferred_element_type=jnp.float32)
        * scaling
    )
    allowed = key_place[None, None, :] <= query_place[None, :, None]
    attend = jnp.where(allowed, jnp.exp(scores - log_norm[:, :, None]), jnp.float32(0.0))
    attend_low = attend.astype(jnp.bfloat16)
    grad_value = jnp.einsum(
        "hqk,qhd->kd", attend_low, grad_heads, preferred_element_type=jnp.float32
    )
    grad_attend = jnp.einsum(
        "qhd,kd->hqk", grad_heads, value_block, preferred_element_type=jnp.float32
    )
    grad_scores = (attend * (grad_attend - deltas[:, :, None])).astype(jnp.bfloat16)
    grad_query = (
        jnp.einsum("hqk,kd->qhd", grad_scores, key_block, preferred_element_type=jnp.float32)
        * scaling
    )
    grad_key = (
        jnp.einsum("hqk,qhd->kd", grad_scores, query_heads, preferred_element_type=jnp.float32)
        * scaling
    )
    return (grad_query, grad_key, grad_value)


def place_tokens(spans, block_len):
    half_len = block_len // 2
    return (spans[:, None] * half_len + jnp.arange(half_len, dtype=jnp.int32)[None, :]).reshape(
        block_len
    )


def local(queries, keys, values, outputs, out_grads, log_sum_exp, span_ids):
    block_len = keys.shape[0]
    head_width = keys.shape[1]
    head_count = log_sum_exp.shape[0]
    query_heads = queries.reshape(block_len, head_count, head_width)
    grad_heads = out_grads.reshape(block_len, head_count, head_width)
    out_heads = outputs.reshape(block_len, head_count, head_width)
    deltas = jnp.sum(grad_heads.astype(jnp.float32) * out_heads.astype(jnp.float32), axis=2).T
    n_inner = lax.axis_size("inner")
    n_outer = lax.axis_size("outer")
    outer_index = lax.axis_index("outer")
    inner_index = lax.axis_index("inner")
    own_block = outer_index * n_inner + inner_index
    query_spans = lax.dynamic_index_in_dim(span_ids, own_block, 1, keepdims=False)
    query_place = place_tokens(query_spans, block_len)

    def block_grads(key_block, value_block, source):
        key_spans = lax.dynamic_index_in_dim(span_ids, source, 1, keepdims=False)
        key_place = place_tokens(key_spans, block_len)
        result = pair_grads(
            query_heads,
            grad_heads,
            log_sum_exp,
            deltas,
            key_block,
            value_block,
            query_place,
            key_place,
        )
        return result

    query_acc, key_acc, value_acc = block_grads(keys, values, own_block)
    key_block, value_block = (keys, values)
    key_carry = jnp.zeros(key_acc.shape, jnp.float32)
    value_carry = jnp.zeros(value_acc.shape, jnp.float32)
    for offset in range(1, INNER_STEPS + 1):
        key_block, value_block = passed_along((key_block, value_block), "inner", 1)
        source = outer_index * n_inner + (inner_index - offset) % n_inner
        grad_query, grad_key, grad_value = block_grads(key_block, value_block, source)
        query_acc = query_acc + grad_query
        if offset > 1:
            key_carry, value_carry = passed_along((key_carry, value_carry), "inner", 1)
        key_carry = key_carry + grad_key
        value_carry = value_carry + grad_value
    back_key, back_value = passed_along((key_carry, value_carry), "inner", -INNER_STEPS)
    key_acc = key_acc + back_key
    value_acc = value_acc + back_value
    key_block, value_block = passed_along((keys, values), "outer", 1)
    source = (outer_index - 1) % n_outer * n_inner + inner_index
    grad_query, grad_key, grad_value = block_grads(key_block, value_block, source)
    query_acc = query_acc + grad_query
    back_key, back_value = passed_along((grad_key, grad_value), "outer", -1)
    key_acc = key_acc + back_key
    value_acc = value_acc + back_value
    return (query_acc.reshape(block_len, head_count * head_width), key_acc, value_acc)


def solution(mesh):
    in_specs = (
        P(("outer", "inner"), None),
        P(("outer", "inner"), None),
        P(("outer", "inner"), None),
        P(("outer", "inner"), None),
        P(("outer", "inner"), None),
        P(None, ("outer", "inner")),
        P(),
    )
    out_specs = (
        P(("outer", "inner"), None),
        P(("outer", "inner"), None),
        P(("outer", "inner"), None),
    )
    return jax.shard_map(local, mesh=mesh, in_specs=in_specs, out_specs=out_specs, check_vma=False)
```

profile of v0, /device:TPU:8, one launch (start us, length us, event | category | flops | bytes accessed | tf_op | source)
XLA Modules:
  0.0 127.3 jit_solution(2166382979428159572)
XLA Ops:
  0.6 4.3 %collective-permute-start.9 = (bf16[256,128]{1,0:T(8,128)(2,1)}, bf16[256,128]{1,0:T(8,128)(2,1)S(1)}, u32[]{:S(2)}, u32[]{:S(2)}) collective-permute-start(bf16[256,128]{1,0:T(8,128)(2,1)} %param.9), channel_id=1, source_target_pairs={{0,32},{32,64},{64,96},{96,128},{128,160},{160,192},{192,224},{224... | collective-permute-start | bytes 196616 | tf_op jit(solution)/shard_map/ppermute | solution.py:12
  5.0 1.9 %collective-permute-start.1 = (bf16[256,128]{1,0:T(8,128)(2,1)}, bf16[256,128]{1,0:T(8,128)(2,1)S(1)}, u32[]{:S(2)}, u32[]{:S(2)}) collective-permute-start(bf16[256,128]{1,0:T(8,128)(2,1)} %param.9), channel_id=1, source_target_pairs={{0,1},{1,2},{2,3},{3,4},{4,5},{5,6},{6,7},{7,8},{8,9},{9,10},{10,1... | collective-permute-start | bytes 196616 | tf_op jit(solution)/shard_map/ppermute | solution.py:12
  6.9 3.5 %collective-permute-start.8 = (bf16[256,128]{1,0:T(8,128)(2,1)}, bf16[256,128]{1,0:T(8,128)(2,1)S(1)}, u32[]{:S(2)}, u32[]{:S(2)}) collective-permute-start(bf16[256,128]{1,0:T(8,128)(2,1)} %param.8), channel_id=1, source_target_pairs={{0,32},{32,64},{64,96},{96,128},{128,160},{160,192},{192,224},{224... | collective-permute-start | bytes 196616 | tf_op jit(solution)/shard_map/ppermute | solution.py:12
  10.4 4.3 %collective-permute-start = (bf16[256,128]{1,0:T(8,128)(2,1)}, bf16[256,128]{1,0:T(8,128)(2,1)S(1)}, u32[]{:S(2)}, u32[]{:S(2)}) collective-permute-start(bf16[256,128]{1,0:T(8,128)(2,1)} %param.8), channel_id=1, source_target_pairs={{0,1},{1,2},{2,3},{3,4},{4,5},{5,6},{6,7},{7,8},{8,9},{9,10},{10,1... | collective-permute-start | bytes 196616 | tf_op jit(solution)/shard_map/ppermute | solution.py:12
  14.8 1.1 copy.105
  16.0 1.1 convert_bitcast_fusion
  18.6 0.6 fusion.23
  19.3 0.4 fusion.21
  20.5 0.4 convolution_bitcast_fusion.5
  21.0 0.6 fusion.19
  21.6 0.4 fusion.17
  22.5 0.5 convolution_bitcast_fusion.4
  23.0 2.2 %collective-permute-start.10 = (f32[256,128]{1,0:T(8,128)S(1)}, f32[256,128]{1,0:T(8,128)S(1)}, u32[]{:S(2)}, u32[]{:S(2)}) collective-permute-start(f32[256,128]{1,0:T(8,128)S(1)} %fusion.31), channel_id=1, source_target_pairs={{0,1},{1,2},{2,3},{3,4},{4,5},{5,6},{6,7},{7,8},{8,9},{9,10},{10,1... | collective-permute-start | bytes 393224 | tf_op jit(solution)/shard_map/ppermute | solution.py:12
  25.2 4.6 %collective-permute-start.15 = (f32[256,128]{1,0:T(8,128)S(1)}, f32[256,128]{1,0:T(8,128)S(1)}, u32[]{:S(2)}, u32[]{:S(2)}) collective-permute-start(f32[256,128]{1,0:T(8,128)S(1)} %convolution_bitcast_fusion.4), channel_id=1, source_target_pairs={{0,1},{1,2},{2,3},{3,4},{4,5},{5,6},{6,7},{7,8},{8,9},{9,10},{10,1... | collective-permute-start | bytes 393224 | tf_op jit(solution)/shard_map/ppermute | solution.py:12
  29.8 0.6 fusion.3
  31.3 3.3 %collective-permute-start.14 = (f32[256,128]{1,0:T(8,128)S(1)}, f32[256,128]{1,0:T(8,128)S(1)}, u32[]{:S(2)}, u32[]{:S(2)}) collective-permute-start(f32[256,128]{1,0:T(8,128)S(1)} %fusion.26), channel_id=1, source_target_pairs={{0,480},{32,0},{64,32},{96,64},{128,96},{160,128},{192,160},{224,1... | collective-permute-start | bytes 393224 | tf_op jit(solution)/shard_map/ppermute | solution.py:12
  34.6 1.9 %collective-permute-start.3 = (bf16[256,128]{1,0:T(8,128)(2,1)S(1)}, bf16[256,128]{1,0:T(8,128)(2,1)S(1)}, u32[]{:S(2)}, u32[]{:S(2)}) collective-permute-start(bf16[256,128]{1,0:T(8,128)(2,1)S(1)} %collective-permute-done.1), channel_id=1, source_target_pairs={{0,1},{1,2},{2,3},{3,4},{4,5},{5,6},{6,7},{7,8},{8,9},{9,10},{10,1... | collective-permute-start | bytes 196616 | tf_op jit(solution)/shard_map/ppermute | solution.py:12
  36.5 2.8 %collective-permute-start.2 = (bf16[256,128]{1,0:T(8,128)(2,1)S(1)}, bf16[256,128]{1,0:T(8,128)(2,1)S(1)}, u32[]{:S(2)}, u32[]{:S(2)}) collective-permute-start(bf16[256,128]{1,0:T(8,128)(2,1)S(1)} %collective-permute-done), channel_id=1, source_target_pairs={{0,1},{1,2},{2,3},{3,4},{4,5},{5,6},{6,7},{7,8},{8,9},{9,10},{10,1... | collective-permute-start | bytes 196616 | tf_op jit(solution)/shard_map/ppermute | solution.py:12
  40.1 0.5 convolution_bitcast_fusion
  40.5 4.0 %collective-permute-done.3 = bf16[256,128]{1,0:T(8,128)(2,1)S(1)} collective-permute-done((bf16[256,128]{1,0:T(8,128)(2,1)S(1)}, bf16[256,128]{1,0:T(8,128)(2,1)S(1)}, u32[]{:S(2)}, u32[]{:S(2)}) %collective-permute-start.3) | collective-permute-done | bytes 65568 | tf_op jit(solution)/shard_map/ppermute | solution.py:12
  44.5 7.4 %collective-permute-start.19 = (f32[256,128]{1,0:T(8,128)S(1)}, f32[256,128]{1,0:T(8,128)S(1)}, u32[]{:S(2)}, u32[]{:S(2)}) collective-permute-start(f32[256,128]{1,0:T(8,128)S(1)} %convolution_bitcast_fusion), channel_id=1, source_target_pairs={{0,480},{32,0},{64,32},{96,64},{128,96},{160,128},{192,160},{224,1... | collective-permute-start | bytes 393224 | tf_op jit(solution)/shard_map/ppermute | solution.py:12
  51.9 1.9 %collective-permute-start.5 = (bf16[256,128]{1,0:T(8,128)(2,1)S(1)}, bf16[256,128]{1,0:T(8,128)(2,1)S(1)}, u32[]{:S(2)}, u32[]{:S(2)}) collective-permute-start(bf16[256,128]{1,0:T(8,128)(2,1)S(1)} %collective-permute-done.3), channel_id=1, source_target_pairs={{0,1},{1,2},{2,3},{3,4},{4,5},{5,6},{6,7},{7,8},{8,9},{9,10},{10,1... | collective-permute-start | bytes 196616 | tf_op jit(solution)/shard_map/ppermute | solution.py:12
  53.9 0.6 fusion.15
  54.5 0.4 fusion.13
  55.3 1.9 %collective-permute-start.4 = (bf16[256,128]{1,0:T(8,128)(2,1)S(1)}, bf16[256,128]{1,0:T(8,128)(2,1)S(1)}, u32[]{:S(2)}, u32[]{:S(2)}) collective-permute-start(bf16[256,128]{1,0:T(8,128)(2,1)S(1)} %collective-permute-done.2), channel_id=1, source_target_pairs={{0,1},{1,2},{2,3},{3,4},{4,5},{5,6},{6,7},{7,8},{8,9},{9,10},{10,1... | collective-permute-start | bytes 196616 | tf_op jit(solution)/shard_map/ppermute | solution.py:12
  57.7 1.9 %collective-permute-start.11 = (f32[256,128]{1,0:T(8,128)S(1)}, f32[256,128]{1,0:T(8,128)S(1)}, u32[]{:S(2)}, u32[]{:S(2)}) collective-permute-start(f32[256,128]{1,0:T(8,128)S(1)} %fusion.30), channel_id=1, source_target_pairs={{0,1},{1,2},{2,3},{3,4},{4,5},{5,6},{6,7},{7,8},{8,9},{9,10},{10,1... | collective-permute-start | bytes 393224 | tf_op jit(solution)/shard_map/ppermute | solution.py:12
  59.6 0.4 fusion.33
  60.1 5.2 %collective-permute-done.4 = bf16[256,128]{1,0:T(8,128)(2,1)S(1)} collective-permute-done((bf16[256,128]{1,0:T(8,128)(2,1)S(1)}, bf16[256,128]{1,0:T(8,128)(2,1)S(1)}, u32[]{:S(2)}, u32[]{:S(2)}) %collective-permute-start.4) | collective-permute-done | bytes 65568 | tf_op jit(solution)/shard_map/ppermute | solution.py:12
  65.2 1.9 %collective-permute-start.16 = (f32[256,128]{1,0:T(8,128)S(1)}, f32[256,128]{1,0:T(8,128)S(1)}, u32[]{:S(2)}, u32[]{:S(2)}) collective-permute-start(f32[256,128]{1,0:T(8,128)S(1)} %fusion.33), channel_id=1, source_target_pairs={{0,1},{1,2},{2,3},{3,4},{4,5},{5,6},{6,7},{7,8},{8,9},{9,10},{10,1... | collective-permute-start | bytes 393224 | tf_op jit(solution)/shard_map/ppermute | solution.py:12
  67.1 0.6 fusion.11
  67.8 0.4 convolution_bitcast_fusion.2
  68.2 0.4 fusion.9
  69.1 2.1 %collective-permute-start.6 = (bf16[256,128]{1,0:T(8,128)(2,1)S(1)}, bf16[256,128]{1,0:T(8,128)(2,1)S(1)}, u32[]{:S(2)}, u32[]{:S(2)}) collective-permute-start(bf16[256,128]{1,0:T(8,128)(2,1)S(1)} %collective-permute-done.4), channel_id=1, source_target_pairs={{0,1},{1,2},{2,3},{3,4},{4,5},{5,6},{6,7},{7,8},{8,9},{9,10},{10,1... | collective-permute-start | bytes 196616 | tf_op jit(solution)/shard_map/ppermute | solution.py:12
  71.6 7.5 %collective-permute-done.6 = bf16[256,128]{1,0:T(8,128)(2,1)S(1)} collective-permute-done((bf16[256,128]{1,0:T(8,128)(2,1)S(1)}, bf16[256,128]{1,0:T(8,128)(2,1)S(1)}, u32[]{:S(2)}, u32[]{:S(2)}) %collective-permute-start.6) | collective-permute-done | bytes 65568 | tf_op jit(solution)/shard_map/ppermute | solution.py:12
  79.1 1.9 %collective-permute-start.7 = (bf16[256,128]{1,0:T(8,128)(2,1)S(1)}, bf16[256,128]{1,0:T(8,128)(2,1)S(1)}, u32[]{:S(2)}, u32[]{:S(2)}) collective-permute-start(bf16[256,128]{1,0:T(8,128)(2,1)S(1)} %collective-permute-done.5), channel_id=1, source_target_pairs={{0,1},{1,2},{2,3},{3,4},{4,5},{5,6},{6,7},{7,8},{8,9},{9,10},{10,1... | collective-permute-start | bytes 196616 | tf_op jit(solution)/shard_map/ppermute | solution.py:12
  81.0 0.6 fusion.7
  81.6 7.4 %collective-permute-done.7 = bf16[256,128]{1,0:T(8,128)(2,1)S(1)} collective-permute-done((bf16[256,128]{1,0:T(8,128)(2,1)S(1)}, bf16[256,128]{1,0:T(8,128)(2,1)S(1)}, u32[]{:S(2)}, u32[]{:S(2)}) %collective-permute-start.7) | collective-permute-done | bytes 65568 | tf_op jit(solution)/shard_map/ppermute | solution.py:12
  89.8 1.9 %collective-permute-start.17 = (f32[256,128]{1,0:T(8,128)S(1)}, f32[256,128]{1,0:T(8,128)S(1)}, u32[]{:S(2)}, u32[]{:S(2)}) collective-permute-start(f32[256,128]{1,0:T(8,128)S(1)} %add.311), channel_id=1, source_target_pairs={{0,1},{1,2},{2,3},{3,4},{4,5},{5,6},{6,7},{7,8},{8,9},{9,10},{10,1... | collective-permute-start | bytes 393224 | tf_op jit(solution)/shard_map/ppermute | solution.py:12
  91.8 0.4 convolution_bitcast_fusion.1
  92.2 1.9 %collective-permute-start.12 = (f32[256,128]{1,0:T(8,128)S(1)}, f32[256,128]{1,0:T(8,128)S(1)}, u32[]{:S(2)}, u32[]{:S(2)}) collective-permute-start(f32[256,128]{1,0:T(8,128)S(1)} %add.306), channel_id=1, source_target_pairs={{0,1},{1,2},{2,3},{3,4},{4,5},{5,6},{6,7},{7,8},{8,9},{9,10},{10,1... | collective-permute-start | bytes 393224 | tf_op jit(solution)/shard_map/ppermute | solution.py:12
  94.2 6.3 %collective-permute-done.17 = f32[256,128]{1,0:T(8,128)S(1)} collective-permute-done((f32[256,128]{1,0:T(8,128)S(1)}, f32[256,128]{1,0:T(8,128)S(1)}, u32[]{:S(2)}, u32[]{:S(2)}) %collective-permute-start.17) | collective-permute-done | bytes 131104 | tf_op jit(solution)/shard_map/ppermute | solution.py:12
  100.5 1.9 %collective-permute-start.18 = (f32[256,128]{1,0:T(8,128)S(1)}, f32[256,128]{1,0:T(8,128)S(1)}, u32[]{:S(2)}, u32[]{:S(2)}) collective-permute-start(f32[256,128]{1,0:T(8,128)S(1)} %add.312), channel_id=1, source_target_pairs={{0,28},{1,29},{2,30},{3,31},{4,0},{5,1},{6,2},{7,3},{8,4},{9,5},{1... | collective-permute-start | bytes 393224 | tf_op jit(solution)/shard_map/ppermute | solution.py:12
  102.8 1.3 %copy.84 = f32[256,1024]{1,0:T(8,128)} copy(f32[256,1024]{0,1:T(8,128)S(1)} %bitcast.325) | data formatting | bytes 2097152
  104.1 11.7 %collective-permute-done.12 = f32[256,128]{1,0:T(8,128)S(1)} collective-permute-done((f32[256,128]{1,0:T(8,128)S(1)}, f32[256,128]{1,0:T(8,128)S(1)}, u32[]{:S(2)}, u32[]{:S(2)}) %collective-permute-start.12) | collective-permute-done | bytes 131104 | tf_op jit(solution)/shard_map/ppermute | solution.py:12
  115.8 1.9 %collective-permute-start.13 = (f32[256,128]{1,0:T(8,128)S(1)}, f32[256,128]{1,0:T(8,128)S(1)}, u32[]{:S(2)}, u32[]{:S(2)}) collective-permute-start(f32[256,128]{1,0:T(8,128)S(1)} %add.307), channel_id=1, source_target_pairs={{0,28},{1,29},{2,30},{3,31},{4,0},{5,1},{6,2},{7,3},{8,4},{9,5},{1... | collective-permute-start | bytes 393224 | tf_op jit(solution)/shard_map/ppermute | solution.py:12
  117.8 0.7 add_add_fusion
  118.5 8.1 %collective-permute-done.13 = f32[256,128]{1,0:T(8,128)S(1)} collective-permute-done((f32[256,128]{1,0:T(8,128)S(1)}, f32[256,128]{1,0:T(8,128)S(1)}, u32[]{:S(2)}, u32[]{:S(2)}) %collective-permute-start.13) | collective-permute-done | bytes 131104 | tf_op jit(solution)/shard_map/ppermute | solution.py:12
  126.6 0.7 add_add_fusion.1
  (51 shorter events, 7.1 us)
Async XLA Ops:
  0.6 18.0 %copy-start = (bf16[256,1024]{1,0:T(8,128)(2,1)S(1)}, bf16[256,1024]{1,0:T(8,128)(2,1)}, u32[]{:S(2)}) copy-start(bf16[256,1024]{1,0:T(8,128)(2,1)} %param.7) | copy-start | bytes 1572868
  0.6 29.8 %collective-permute-start.9 = (bf16[256,128]{1,0:T(8,128)(2,1)}, bf16[256,128]{1,0:T(8,128)(2,1)S(1)}, u32[]{:S(2)}, u32[]{:S(2)}) collective-permute-start(bf16[256,128]{1,0:T(8,128)(2,1)} %param.9), channel_id=1, source_target_pairs={{0,32},{32,64},{64,96},{96,128},{128,160},{160,192},{192,224},{224... | collective-permute-start | bytes 196616 | tf_op jit(solution)/shard_map/ppermute | solution.py:12
  5.0 16.7 %collective-permute-start.1 = (bf16[256,128]{1,0:T(8,128)(2,1)}, bf16[256,128]{1,0:T(8,128)(2,1)S(1)}, u32[]{:S(2)}, u32[]{:S(2)}) collective-permute-start(bf16[256,128]{1,0:T(8,128)(2,1)} %param.9), channel_id=1, source_target_pairs={{0,1},{1,2},{2,3},{3,4},{4,5},{5,6},{6,7},{7,8},{8,9},{9,10},{10,1... | collective-permute-start | bytes 196616 | tf_op jit(solution)/shard_map/ppermute | solution.py:12
  6.9 22.9 %collective-permute-start.8 = (bf16[256,128]{1,0:T(8,128)(2,1)}, bf16[256,128]{1,0:T(8,128)(2,1)S(1)}, u32[]{:S(2)}, u32[]{:S(2)}) collective-permute-start(bf16[256,128]{1,0:T(8,128)(2,1)} %param.8), channel_id=1, source_target_pairs={{0,32},{32,64},{64,96},{96,128},{128,160},{160,192},{192,224},{224... | collective-permute-start | bytes 196616 | tf_op jit(solution)/shard_map/ppermute | solution.py:12
  10.4 10.6 %collective-permute-start = (bf16[256,128]{1,0:T(8,128)(2,1)}, bf16[256,128]{1,0:T(8,128)(2,1)S(1)}, u32[]{:S(2)}, u32[]{:S(2)}) collective-permute-start(bf16[256,128]{1,0:T(8,128)(2,1)} %param.8), channel_id=1, source_target_pairs={{0,1},{1,2},{2,3},{3,4},{4,5},{5,6},{6,7},{7,8},{8,9},{9,10},{10,1... | collective-permute-start | bytes 196616 | tf_op jit(solution)/shard_map/ppermute | solution.py:12
  17.1 0.7 copy-start.4
  17.1 1.5 %copy-start.3 = (bf16[256,128]{1,0:T(8,128)(2,1)S(1)}, bf16[256,128]{1,0:T(8,128)(2,1)}, u32[]{:S(2)}) copy-start(bf16[256,128]{1,0:T(8,128)(2,1)} %param.8) | copy-start | bytes 196612
  17.2 1.5 %copy-start.5 = (f32[8,256]{1,0:T(8,128)S(1)}, f32[8,256]{1,0:T(8,128)}, u32[]{:S(2)}) copy-start(f32[8,256]{1,0:T(8,128)} %param.12) | copy-start | bytes 24580
  17.7 1.5 %copy-start.1 = (bf16[256,1024]{1,0:T(8,128)(2,1)S(1)}, bf16[256,1024]{1,0:T(8,128)(2,1)}, u32[]{:S(2)}) copy-start(bf16[256,1024]{1,0:T(8,128)(2,1)} %param.11) | copy-start | bytes 1572868
  17.7 1.5 %copy-start.2 = (bf16[256,128]{1,0:T(8,128)(2,1)S(1)}, bf16[256,128]{1,0:T(8,128)(2,1)}, u32[]{:S(2)}) copy-start(bf16[256,128]{1,0:T(8,128)(2,1)} %param.9) | copy-start | bytes 196612
  23.0 32.4 %collective-permute-start.10 = (f32[256,128]{1,0:T(8,128)S(1)}, f32[256,128]{1,0:T(8,128)S(1)}, u32[]{:S(2)}, u32[]{:S(2)}) collective-permute-start(f32[256,128]{1,0:T(8,128)S(1)} %fusion.31), channel_id=1, source_target_pairs={{0,1},{1,2},{2,3},{3,4},{4,5},{5,6},{6,7},{7,8},{8,9},{9,10},{10,1... | collective-permute-start | bytes 393224 | tf_op jit(solution)/shard_map/ppermute | solution.py:12
  25.2 32.5 %collective-permute-start.15 = (f32[256,128]{1,0:T(8,128)S(1)}, f32[256,128]{1,0:T(8,128)S(1)}, u32[]{:S(2)}, u32[]{:S(2)}) collective-permute-start(f32[256,128]{1,0:T(8,128)S(1)} %convolution_bitcast_fusion.4), channel_id=1, source_target_pairs={{0,1},{1,2},{2,3},{3,4},{4,5},{5,6},{6,7},{7,8},{8,9},{9,10},{10,1... | collective-permute-start | bytes 393224 | tf_op jit(solution)/shard_map/ppermute | solution.py:12
  31.3 87.1 %collective-permute-start.14 = (f32[256,128]{1,0:T(8,128)S(1)}, f32[256,128]{1,0:T(8,128)S(1)}, u32[]{:S(2)}, u32[]{:S(2)}) collective-permute-start(f32[256,128]{1,0:T(8,128)S(1)} %fusion.26), channel_id=1, source_target_pairs={{0,480},{32,0},{64,32},{96,64},{128,96},{160,128},{192,160},{224,1... | collective-permute-start | bytes 393224 | tf_op jit(solution)/shard_map/ppermute | solution.py:12
  34.6 9.9 %collective-permute-start.3 = (bf16[256,128]{1,0:T(8,128)(2,1)S(1)}, bf16[256,128]{1,0:T(8,128)(2,1)S(1)}, u32[]{:S(2)}, u32[]{:S(2)}) collective-permute-start(bf16[256,128]{1,0:T(8,128)(2,1)S(1)} %collective-permute-done.1), channel_id=1, source_target_pairs={{0,1},{1,2},{2,3},{3,4},{4,5},{5,6},{6,7},{7,8},{8,9},{9,10},{10,1... | collective-permute-start | bytes 196616 | tf_op jit(solution)/shard_map/ppermute | solution.py:12
  36.5 15.4 %collective-permute-start.2 = (bf16[256,128]{1,0:T(8,128)(2,1)S(1)}, bf16[256,128]{1,0:T(8,128)(2,1)S(1)}, u32[]{:S(2)}, u32[]{:S(2)}) collective-permute-start(bf16[256,128]{1,0:T(8,128)(2,1)S(1)} %collective-permute-done), channel_id=1, source_target_pairs={{0,1},{1,2},{2,3},{3,4},{4,5},{5,6},{6,7},{7,8},{8,9},{9,10},{10,1... | collective-permute-start | bytes 196616 | tf_op jit(solution)/shard_map/ppermute | solution.py:12
  44.5 73.3 %collective-permute-start.19 = (f32[256,128]{1,0:T(8,128)S(1)}, f32[256,128]{1,0:T(8,128)S(1)}, u32[]{:S(2)}, u32[]{:S(2)}) collective-permute-start(f32[256,128]{1,0:T(8,128)S(1)} %convolution_bitcast_fusion), channel_id=1, source_target_pairs={{0,480},{32,0},{64,32},{96,64},{128,96},{160,128},{192,160},{224,1... | collective-permute-start | bytes 393224 | tf_op jit(solution)/shard_map/ppermute | solution.py:12
  51.9 16.3 %collective-permute-start.5 = (bf16[256,128]{1,0:T(8,128)(2,1)S(1)}, bf16[256,128]{1,0:T(8,128)(2,1)S(1)}, u32[]{:S(2)}, u32[]{:S(2)}) collective-permute-start(bf16[256,128]{1,0:T(8,128)(2,1)S(1)} %collective-permute-done.3), channel_id=1, source_target_pairs={{0,1},{1,2},{2,3},{3,4},{4,5},{5,6},{6,7},{7,8},{8,9},{9,10},{10,1... | collective-permute-start | bytes 196616 | tf_op jit(solution)/shard_map/ppermute | solution.py:12
  55.3 9.9 %collective-permute-start.4 = (bf16[256,128]{1,0:T(8,128)(2,1)S(1)}, bf16[256,128]{1,0:T(8,128)(2,1)S(1)}, u32[]{:S(2)}, u32[]{:S(2)}) collective-permute-start(bf16[256,128]{1,0:T(8,128)(2,1)S(1)} %collective-permute-done.2), channel_id=1, source_target_pairs={{0,1},{1,2},{2,3},{3,4},{4,5},{5,6},{6,7},{7,8},{8,9},{9,10},{10,1... | collective-permute-start | bytes 196616 | tf_op jit(solution)/shard_map/ppermute | solution.py:12
  57.7 34.5 %collective-permute-start.11 = (f32[256,128]{1,0:T(8,128)S(1)}, f32[256,128]{1,0:T(8,128)S(1)}, u32[]{:S(2)}, u32[]{:S(2)}) collective-permute-start(f32[256,128]{1,0:T(8,128)S(1)} %fusion.30), channel_id=1, source_target_pairs={{0,1},{1,2},{2,3},{3,4},{4,5},{5,6},{6,7},{7,8},{8,9},{9,10},{10,1... | collective-permute-start | bytes 393224 | tf_op jit(solution)/shard_map/ppermute | solution.py:12
  65.2 24.6 %collective-permute-start.16 = (f32[256,128]{1,0:T(8,128)S(1)}, f32[256,128]{1,0:T(8,128)S(1)}, u32[]{:S(2)}, u32[]{:S(2)}) collective-permute-start(f32[256,128]{1,0:T(8,128)S(1)} %fusion.33), channel_id=1, source_target_pairs={{0,1},{1,2},{2,3},{3,4},{4,5},{5,6},{6,7},{7,8},{8,9},{9,10},{10,1... | collective-permute-start | bytes 393224 | tf_op jit(solution)/shard_map/ppermute | solution.py:12
  69.1 10.0 %collective-permute-start.6 = (bf16[256,128]{1,0:T(8,128)(2,1)S(1)}, bf16[256,128]{1,0:T(8,128)(2,1)S(1)}, u32[]{:S(2)}, u32[]{:S(2)}) collective-permute-start(bf16[256,128]{1,0:T(8,128)(2,1)S(1)} %collective-permute-done.4), channel_id=1, source_target_pairs={{0,1},{1,2},{2,3},{3,4},{4,5},{5,6},{6,7},{7,8},{8,9},{9,10},{10,1... | collective-permute-start | bytes 196616 | tf_op jit(solution)/shard_map/ppermute | solution.py:12
  79.1 9.9 %collective-permute-start.7 = (bf16[256,128]{1,0:T(8,128)(2,1)S(1)}, bf16[256,128]{1,0:T(8,128)(2,1)S(1)}, u32[]{:S(2)}, u32[]{:S(2)}) collective-permute-start(bf16[256,128]{1,0:T(8,128)(2,1)S(1)} %collective-permute-done.5), channel_id=1, source_target_pairs={{0,1},{1,2},{2,3},{3,4},{4,5},{5,6},{6,7},{7,8},{8,9},{9,10},{10,1... | collective-permute-start | bytes 196616 | tf_op jit(solution)/shard_map/ppermute | solution.py:12
  89.8 10.6 %collective-permute-start.17 = (f32[256,128]{1,0:T(8,128)S(1)}, f32[256,128]{1,0:T(8,128)S(1)}, u32[]{:S(2)}, u32[]{:S(2)}) collective-permute-start(f32[256,128]{1,0:T(8,128)S(1)} %add.311), channel_id=1, source_target_pairs={{0,1},{1,2},{2,3},{3,4},{4,5},{5,6},{6,7},{7,8},{8,9},{9,10},{10,1... | collective-permute-start | bytes 393224 | tf_op jit(solution)/shard_map/ppermute | solution.py:12
  92.2 23.6 %collective-permute-start.12 = (f32[256,128]{1,0:T(8,128)S(1)}, f32[256,128]{1,0:T(8,128)S(1)}, u32[]{:S(2)}, u32[]{:S(2)}) collective-permute-start(f32[256,128]{1,0:T(8,128)S(1)} %add.306), channel_id=1, source_target_pairs={{0,1},{1,2},{2,3},{3,4},{4,5},{5,6},{6,7},{7,8},{8,9},{9,10},{10,1... | collective-permute-start | bytes 393224 | tf_op jit(solution)/shard_map/ppermute | solution.py:12
  100.5 17.3 %collective-permute-start.18 = (f32[256,128]{1,0:T(8,128)S(1)}, f32[256,128]{1,0:T(8,128)S(1)}, u32[]{:S(2)}, u32[]{:S(2)}) collective-permute-start(f32[256,128]{1,0:T(8,128)S(1)} %add.312), channel_id=1, source_target_pairs={{0,28},{1,29},{2,30},{3,31},{4,0},{5,1},{6,2},{7,3},{8,4},{9,5},{1... | collective-permute-start | bytes 393224 | tf_op jit(solution)/shard_map/ppermute | solution.py:12
  115.8 10.8 %collective-permute-start.13 = (f32[256,128]{1,0:T(8,128)S(1)}, f32[256,128]{1,0:T(8,128)S(1)}, u32[]{:S(2)}, u32[]{:S(2)}) collective-permute-start(f32[256,128]{1,0:T(8,128)S(1)} %add.307), channel_id=1, source_target_pairs={{0,28},{1,29},{2,30},{3,31},{4,0},{5,1},{6,2},{7,3},{8,4},{9,5},{1... | collective-permute-start | bytes 393224 | tf_op jit(solution)/shard_map/ppermute | solution.py:12
where the time goes:
time: 128 us; the launch traced here: 127 us
  starting transfers between devices  55.6 us (43%)
  waiting for transfers between devices  50.1 us (39%)
  matrix products  13.7 us (11%)
  other arithmetic  3.69 us (3%)
  local copies, waits for them, and re-layouts  2.74 us (2%)
  between operations  1.35 us (1%)
    ppermute x20, starting transfers between devices, passed_along(): return lax.ppermute(value, axis, pairs)  55.6 us
    ppermute x20, waiting for transfers between devices, passed_along(): return lax.ppermute(value, axis, pairs)  50.1 us
    dot_general x6, matrix products, pair_grads(): jnp.einsum('qhd,kd->hqk', query_heads, key_block, preferred_element_type=...  3.69 us
    dot_general x6, matrix products, pair_grads(): jnp.einsum('hqk,qhd->kd', attend_low, grad_heads, preferred_element_type=...  2.7 us
    unnamed x15, local copies, waits for them, and re-layouts  2.69 us
    dot_general x6, matrix products, pair_grads(): jnp.einsum('qhd,kd->hqk', grad_heads, value_block, preferred_element_type...  2.65 us
    dot_general x6, matrix products, pair_grads(): jnp.einsum('hqk,qhd->kd', grad_scores, query_heads, preferred_element_typ...  2.58 us
  transfers between devices with their start and end apart: 20, of which 7 were waited for; matrix products, arithmetic and copies ran while one was open for 15% of the time, Pallas kernels for 0%

commit v1 on v0

v1 whole, which is shorter than its diff:
```python
import functools
import math

import jax
import jax.numpy as jnp
from jax import lax
from jax.experimental import pallas as pl
from jax.experimental.pallas import tpu as pltpu
from jax.sharding import PartitionSpec as P

MESH = pl.DeviceIdType.MESH
HALF = 128
DIM = 128
HEADS = 8
PAIR = 256
NT = (((1,), (1,)), ((), ()))
NN = (((1,), (0,)), ((), ()))
TN = (((0,), (0,)), ((), ()))
LOG2E = math.log2(math.e)

OWN, TWO, FOUR, ONE, THREE, OUTER = range(6)


def dot(a, b, dims):
    return lax.dot_general(a, b, dims, preferred_element_type=jnp.float32)


def kernel(
    n_outer,
    n_inner,
    spans,
    q_hbm,
    k_hbm,
    v_hbm,
    o_hbm,
    g_hbm,
    lse_hbm,
    dq_hbm,
    dk_hbm,
    dv_hbm,
    q_in,
    k_in,
    v_in,
    o_in,
    g_in,
    lse_in,
    qn,
    gn,
    rows,
    kv,
    dq,
    acc,
    own_acc,
    gout,
    gin,
    dq_out,
    dkv_out,
    load_sem,
    store_sem,
    kv_send,
    kv_recv,
    g_send,
    g_recv,
):
    outer = lax.axis_index("outer")
    inner = lax.axis_index("inner")
    core = lax.rem(inner, 2)
    scale = DIM ** (-0.5)

    def at(do, di):
        return (lax.rem(outer + do + n_outer, n_outer), lax.rem(inner + di + n_inner, n_inner))

    partner = (outer, inner + 1 - 2 * core)
    friends = [at(0, 2), at(0, -2), at(0, 4), at(0, -4), at(1, 0), at(-1, 0), partner]

    loads = [
        pltpu.make_async_copy(src, dst, load_sem.at[n])
        for n, (src, dst) in enumerate(
            [
                (k_hbm, k_in),
                (v_hbm, v_in),
                (g_hbm, g_in),
                (o_hbm, o_in),
                (q_hbm, q_in),
                (lse_hbm, lse_in),
            ]
        )
    ]
    for copy in loads:
        copy.start()

    barrier = pltpu.get_barrier_semaphore()
    for friend in friends:
        pl.semaphore_signal(barrier, inc=1, device_id=friend, device_id_type=MESH)

    def low_span(block):
        return jnp.minimum(spans[0, block], spans[1, block])

    def less(a, b, shape):
        return jnp.full(shape, a, jnp.int32) < jnp.full(shape, b, jnp.int32)

    def narrow(mask):
        return jnp.where(mask, 1.0, 0.0).astype(jnp.bfloat16) > 0.5

    def either(mask, yes, no):
        return jnp.where(mask, yes, no)

    own_block = outer * n_inner + inner
    own_low = low_span(own_block)
    swapped = less(spans[1, own_block], spans[0, own_block], (HALF, DIM))
    swapped_low = narrow(swapped)

    def by_span(first, second, half, mask):
        return either(mask, *((second, first) if half == 0 else (first, second)))

    def kv_copy(part, slot_from, slot_to, number, target):
        return pltpu.make_async_remote_copy(
            src_ref=kv.at[slot_from, part],
            dst_ref=kv.at[slot_to, part],
            send_sem=kv_send.at[number, part],
            recv_sem=kv_recv.at[slot_to, part],
            device_id=target,
            device_id_type=MESH,
        )

    to_four = [kv_copy(p, OWN, FOUR, 0, at(0, 4)) for p in range(2)]
    to_two = [kv_copy(p, OWN, TWO, 1, at(0, 2)) for p in range(2)]
    to_outer = [kv_copy(p, OWN, OUTER, 2, at(1, 0)) for p in range(2)]
    to_one = [kv_copy(p, core, ONE, 3, partner) for p in range(2)]
    to_three = [kv_copy(p, core + 1, THREE, 4, partner) for p in range(2)]

    for part, (copy, ref) in enumerate([(loads[0], k_in), (loads[1], v_in)]):
        copy.wait()
        for half in range(2):
            kv[OWN, part, pl.ds(half * HALF, HALF), :] = by_span(
                ref[:HALF, :], ref[HALF:, :], half, swapped_low
            )
    pl.semaphore_wait(barrier, len(friends))
    for part in range(2):
        to_four[part].start()
        to_two[part].start()
        to_outer[part].start()

        @pl.when(core == 0)
        def _():
            to_one[part].start()

    for copy in loads[2:]:
        copy.wait()
    ones = jnp.ones((8, DIM), jnp.bfloat16)
    for half in range(2):

        def prepare(h, carry, half=half):
            col = pl.ds(pl.multiple_of(h * DIM, DIM), DIM)

            def halved(ref):
                return by_span(ref[pl.ds(0, HALF), col], ref[pl.ds(HALF, HALF), col], half, swapped_low)

            grad = halved(g_in)
            qn[half, col, :] = halved(q_in)
            gn[half, col, :] = grad
            product = grad.astype(jnp.float32) * halved(o_in).astype(jnp.float32)
            top = product.astype(jnp.bfloat16)
            rest = product - top.astype(jnp.float32)
            middle = rest.astype(jnp.bfloat16)
            low = (rest - middle.astype(jnp.float32)).astype(jnp.bfloat16)
            delta = dot(ones, top, NT) + dot(ones, middle, NT) + dot(ones, low, NT)
            rows[half, 0:1, col] = delta[0:1, :]
            return carry

        lax.fori_loop(0, HEADS, prepare, 0)
        for h in range(HEADS):
            rows[half, 1:2, pl.ds(h * DIM, DIM)] = LOG2E * by_span(
                lse_in[h : h + 1, :HALF], lse_in[h : h + 1, HALF:], half, swapped[:1]
            )

    def attend(keys, q, norm):
        return jnp.exp2(dot(keys, q, NT) * (scale * LOG2E) - norm)

    def score_grads(p, values, g, delta):
        return (p * (dot(values, g, NT) - delta)).astype(jnp.bfloat16)

    key_at = lax.broadcasted_iota(jnp.int32, (HALF, PAIR), 0)
    query_at = lax.rem(lax.broadcasted_iota(jnp.int32, (HALF, PAIR), 1), HALF)
    seen = key_at <= query_at
    own_acc[...] = jnp.zeros_like(own_acc)

    def own_step(step, carry):
        cols = pl.ds(pl.multiple_of(step * PAIR, PAIR), PAIR)
        keys = kv[OWN, 0]
        values = kv[OWN, 1]
        q_lo, q_hi = qn[0, cols, :], qn[1, cols, :]
        g_lo, g_hi = gn[0, cols, :], gn[1, cols, :]
        p_lo = jnp.where(seen, attend(keys[:HALF], q_lo, rows[0, 1:2, cols]), 0.0)
        p_hi = attend(keys, q_hi, rows[1, 1:2, cols])
        p_hi = jnp.concatenate([p_hi[:HALF], jnp.where(seen, p_hi[HALF:], 0.0)], 0)
        own_acc[1] += dot(p_hi.astype(jnp.bfloat16), g_hi, NN)
        own_acc[1, pl.ds(0, HALF), :] += dot(p_lo.astype(jnp.bfloat16), g_lo, NN)
        s_lo = score_grads(p_lo, values[:HALF], g_lo, rows[0, 0:1, cols])
        s_hi = score_grads(p_hi, values, g_hi, rows[1, 0:1, cols])
        own_acc[0] += dot(s_hi, q_hi, NN)
        own_acc[0, pl.ds(0, HALF), :] += dot(s_lo, q_lo, NN)
        dq[cols, pl.ds(0, DIM)] = dot(s_lo, keys[:HALF], TN)
        dq[cols, pl.ds(DIM, DIM)] = dot(s_hi, keys, TN)
        return carry

    lax.fori_loop(0, HEADS * HALF // PAIR, own_step, 0)

    def other(slot, block):
        early = less(low_span(block), own_low, (HALF, DIM))
        early_low = narrow(less(low_span(block), own_low, (PAIR, DIM)))
        early_row = less(low_span(block), own_low, (1, PAIR))
        acc[...] = jnp.zeros_like(acc)

        def step_of(step, carry):
            cols = pl.ds(pl.multiple_of(step * PAIR, PAIR), PAIR)
            k1, v1 = kv[slot, 0, pl.ds(0, HALF), :], kv[slot, 1, pl.ds(0, HALF), :]
            k2 = either(early_low[:HALF], k1, kv[slot, 0, pl.ds(HALF, HALF), :])
            v2 = either(early_low[:HALF], v1, kv[slot, 1, pl.ds(HALF, HALF), :])
            q1, g1 = qn[1, cols, :], gn[1, cols, :]
            q2 = either(early_low, qn[0, cols, :], q1)
            g2 = either(early_low, gn[0, cols, :], g1)
            norm1, delta1 = rows[1, 1:2, cols], rows[1, 0:1, cols]
            norm2 = either(early_row, rows[0, 1:2, cols], norm1)
            delta2 = either(early_row, rows[0, 0:1, cols], delta1)
            p1 = attend(k1, q1, norm1)
            p2 = attend(k2, q2, norm2)
            acc[0, 1] += dot(p1.astype(jnp.bfloat16), g1, NN)
            acc[1, 1] += dot(p2.astype(jnp.bfloat16), g2, NN)
            s1 = score_grads(p1, v1, g1, delta1)
            s2 = score_grads(p2, v2, g2, delta2)
            acc[0, 0] += dot(s1, q1, NN)
            acc[1, 0] += dot(s2, q2, NN)
            zero = jnp.zeros_like(k1)
            wide = jnp.concatenate(
                [
                    jnp.concatenate([zero, k1], 1),
                    jnp.concatenate(
                        [either(early_low[:HALF], k2, zero), either(early_low[:HALF], zero, k2)], 1
                    ),
                ],
                0,
            )
            dq[cols, :] += dot(jnp.concatenate([s1, s2], 0), wide, TN)
            return carry

        lax.fori_loop(0, HEADS * HALF // PAIR, step_of, 0)
        result = []
        for part in range(2):
            first, second = acc[0, part], acc[1, part]
            result.append(
                (
                    first + jnp.where(early, second, 0.0),
                    jnp.where(early, 0.0, second),
                )
            )
        return result

    def block_at(do, di):
        there = at(do, di)
        return there[0] * n_inner + there[1]

    def put(slot, grads, extra=None):
        for part in range(2):
            for half in range(2):
                where = pl.ds(half * HALF, HALF)
                value = grads[part][half]
                if extra is not None:
                    value = value + gin[extra, part, where, :].astype(jnp.float32)
                gout[slot, part, where, :] = value.astype(jnp.bfloat16)

    def g_copy(slot, target):
        return pltpu.make_async_remote_copy(
            src_ref=gout.at[slot],
            dst_ref=gin.at[slot],
            send_sem=g_send.at[slot],
            recv_sem=g_recv.at[slot],
            device_id=target,
            device_id_type=MESH,
        )

    g_two = g_copy(TWO, at(0, -2))
    g_four = g_copy(FOUR, at(0, -4))
    g_outer = g_copy(OUTER, at(-1, 0))
    g_one = g_copy(ONE, partner)
    g_three = g_copy(THREE, partner)

    def add_to(slot, extra):
        gout[slot] = (gout[slot].astype(jnp.float32) + gin[extra].astype(jnp.float32)).astype(
            jnp.bfloat16
        )

    def both_recv(copies):
        for copy in copies:
            copy.wait_recv()

    both_recv(to_two)

    @pl.when(core == 0)
    def _():
        for copy in to_three:
            copy.start()

    @pl.when(core == 1)
    def _():
        for copy in to_one:
            copy.start()

    both_recv(to_outer)
    put(OUTER, other(OUTER, block_at(-1, 0)))
    g_outer.start()
    both_recv(to_four)

    @pl.when(core == 1)
    def _():
        for copy in to_three:
            copy.start()

    put(TWO, other(TWO, block_at(0, -2)))
    both_recv(to_one)
    put(ONE, other(ONE, block_at(0, -1)))
    g_one.start()
    both_recv(to_three)
    put(THREE, other(THREE, block_at(0, -3)))
    g_three.start()
    put(FOUR, other(FOUR, block_at(0, -4)))
    g_one.wait_recv()
    g_three.wait_recv()

    @pl.when(core == 0)
    def _():
        add_to(TWO, THREE)

    @pl.when(core == 1)
    def _():
        add_to(TWO, ONE)
        add_to(FOUR, THREE)

    g_four.start()
    g_two.start()

    for half in range(2):

        def finish(h, carry, half=half):
            head = pl.ds(pl.multiple_of(h * DIM, DIM), DIM)
            value = by_span(dq[head, pl.ds(0, DIM)], dq[head, pl.ds(DIM, DIM)], half, swapped)
            dq_out[pl.ds(half * HALF, HALF), head] = value * scale
            return carry

        lax.fori_loop(0, HEADS, finish, 0)
    store_dq = pltpu.make_async_copy(dq_out, dq_hbm, store_sem.at[0])
    store_dq.start()

    @pl.when(core == 0)
    def _():
        for part in range(2):
            own_acc[part] += gin[ONE, part].astype(jnp.float32)

    g_outer.wait_recv()
    g_two.wait_recv()
    g_four.wait_recv()
    for part in range(2):
        total = own_acc[part]
        for slot in (OUTER, TWO, FOUR):
            total = total + gin[slot, part].astype(jnp.float32)
        if part == 0:
            total = total * scale
        lo, hi = total[:HALF], total[HALF:]
        dkv_out[part, pl.ds(0, HALF), :] = by_span(lo, hi, 0, swapped)
        dkv_out[part, pl.ds(HALF, HALF), :] = by_span(lo, hi, 1, swapped)
    stores = [
        pltpu.make_async_copy(dkv_out.at[0], dk_hbm, store_sem.at[1]),
        pltpu.make_async_copy(dkv_out.at[1], dv_hbm, store_sem.at[2]),
    ]
    for copy in stores:
        copy.start()
    for copies in (to_four, to_two, to_outer, to_one, to_three):
        for copy in copies:
            copy.wait_send()
    for copy in (g_two, g_four, g_outer, g_one, g_three):
        copy.wait_send()
    store_dq.wait()
    for copy in stores:
        copy.wait()


def local(n_outer, n_inner, queries, keys, values, outputs, out_grads, log_sum_exp, span_ids):
    block, dim = keys.shape
    width = queries.shape[1]
    heads = log_sum_exp.shape[0]
    bf16, f32 = jnp.bfloat16, jnp.float32
    in_hbm = pl.BlockSpec(memory_space=pl.ANY)
    return pl.pallas_call(
        functools.partial(kernel, n_outer, n_inner),
        out_shape=(
            jax.ShapeDtypeStruct((block, width), f32),
            jax.ShapeDtypeStruct((block, dim), f32),
            jax.ShapeDtypeStruct((block, dim), f32),
        ),
        in_specs=[pl.BlockSpec(memory_space=pltpu.SMEM)] + [in_hbm] * 6,
        out_specs=(in_hbm,) * 3,
        scratch_shapes=[
            pltpu.VMEM((block, width), bf16),
            pltpu.VMEM((block, dim), bf16),
            pltpu.VMEM((block, dim), bf16),
            pltpu.VMEM((block, width), bf16),
            pltpu.VMEM((block, width), bf16),
            pltpu.VMEM((heads, block), f32),
            pltpu.VMEM((2, heads * HALF, dim), bf16),
            pltpu.VMEM((2, heads * HALF, dim), bf16),
            pltpu.VMEM((2, 8, heads * HALF), f32),
            pltpu.VMEM((6, 2, block, dim), bf16),
            pltpu.VMEM((heads * HALF, 2 * dim), f32),
            pltpu.VMEM((2, 2, HALF, dim), f32),
            pltpu.VMEM((2, block, dim), f32),
            pltpu.VMEM((6, 2, block, dim), bf16),
            pltpu.VMEM((6, 2, block, dim), bf16),
            pltpu.VMEM((block, width), f32),
            pltpu.VMEM((2, block, dim), f32),
            pltpu.SemaphoreType.DMA((6,)),
            pltpu.SemaphoreType.DMA((3,)),
            pltpu.SemaphoreType.DMA((5, 2)),
            pltpu.SemaphoreType.DMA((6, 2)),
            pltpu.SemaphoreType.DMA((6,)),
            pltpu.SemaphoreType.DMA((6,)),
        ],
        compiler_params=pltpu.CompilerParams(
            collective_id=0, has_side_effects=True, vmem_limit_bytes=40 * 1024 * 1024
        ),
        name="backward",
    )(span_ids, queries, keys, values, outputs, out_grads, log_sum_exp)


def solution(mesh):
    tokens = P(("outer", "inner"), None)
    return jax.shard_map(
        functools.partial(local, mesh.shape["outer"], mesh.shape["inner"]),
        mesh=mesh,
        in_specs=(tokens,) * 5 + (P(None, ("outer", "inner")), P()),
        out_specs=(tokens,) * 3,
        check_vma=False,
    )
```

time: 128 us -> 61.1 us (0.48)
  the two profiles are of different devices: /device:TPU:8 before, /device:TPU:14 now
where the time goes in v1:
time: 61.1 us; the launch traced here: 60.7 us
  Pallas kernels  51.6 us (84%)
  local copies, waits for them, and re-layouts  8.46 us (14%)
  between operations  0.66 us (1%)
    pallas_call x1, Pallas kernels, local(): pl.pallas_call(functools.partial(kernel, n_outer, n_inner), out_shape=(ja...  51.6 us
    unnamed x17, local copies, waits for them, and re-layouts  8.46 us

profile of v1, /device:TPU:14, one launch (start us, length us, event | category | flops | bytes accessed | tf_op | source)
XLA Modules:
  0.0 60.7 jit_solution(5589431868543092693)
XLA Ops:
  0.6 0.0 copy-start
  0.6 1.0 %copy-done = bf16[256,1024]{1,0:T(8,128)(2,1)S(1)} copy-done((bf16[256,1024]{1,0:T(8,128)(2,1)S(1)}, bf16[256,1024]{1,0:T(8,128)(2,1)}, u32[]{:S(2)}) %copy-start) | copy-done | bytes 524312
  1.7 0.0 copy-start.1
  1.7 1.0 %copy-done.1 = bf16[256,1024]{1,0:T(8,128)(2,1)S(1)} copy-done((bf16[256,1024]{1,0:T(8,128)(2,1)S(1)}, bf16[256,1024]{1,0:T(8,128)(2,1)}, u32[]{:S(2)}) %copy-start.1) | copy-done | bytes 524312
  2.7 0.0 copy-start.2
  2.7 1.0 %copy-done.2 = bf16[256,1024]{1,0:T(8,128)(2,1)S(1)} copy-done((bf16[256,1024]{1,0:T(8,128)(2,1)S(1)}, bf16[256,1024]{1,0:T(8,128)(2,1)}, u32[]{:S(2)}) %copy-start.2) | copy-done | bytes 524312
  3.8 0.0 copy-start.3
  3.8 0.8 %copy-done.3 = bf16[256,128]{1,0:T(8,128)(2,1)S(1)} copy-done((bf16[256,128]{1,0:T(8,128)(2,1)S(1)}, bf16[256,128]{1,0:T(8,128)(2,1)}, u32[]{:S(2)}) %copy-start.3) | copy-done | bytes 65560
  4.6 0.0 copy-start.4
  4.6 0.8 %copy-done.4 = bf16[256,128]{1,0:T(8,128)(2,1)S(1)} copy-done((bf16[256,128]{1,0:T(8,128)(2,1)S(1)}, bf16[256,128]{1,0:T(8,128)(2,1)}, u32[]{:S(2)}) %copy-start.4) | copy-done | bytes 65560
  5.4 0.0 copy-start.5
  5.4 0.7 %copy-done.5 = f32[8,256]{1,0:T(8,128)S(1)} copy-done((f32[8,256]{1,0:T(8,128)S(1)}, f32[8,256]{1,0:T(8,128)}, u32[]{:S(2)}) %copy-start.5) | copy-done | bytes 8216
  6.1 0.0 copy-start.6
  6.1 0.7 %copy-done.6 = s32[2,512]{1,0:T(2,128)S(1)} copy-done((s32[2,512]{1,0:T(2,128)S(1)}, s32[2,512]{1,0:T(2,128)}, u32[]{:S(2)}) %copy-start.6) | copy-done | bytes 4120
  6.8 51.6 %backward.1 = (f32[256,1024]{1,0:T(8,128)S(1)}, f32[256,128]{1,0:T(8,128)S(1)}, f32[256,128]{1,0:T(8,128)S(1)}) custom-call(s32[2,512]{1,0:T(2,128)S(1)} %copy-done.6, bf16[256,1024]{1,0:T(8,128)(2,1)S(1)} %copy-done, bf16[256,128]{1,0:T(8,128)(2,1)S(1)} %copy-done.3, bf16[256,128]{1,0:T(8,128)(2,1)S(1)} %copy-done.4, bf16[256,1024]{1,0:T(8,128)(2,1)S(1)} %copy-done.1, ...), custom_call_target="tpu_custom_call" | custom-call | tf_op jit(solution)/shard_map/backward/pallas_call | solution.py:393
  58.4 1.0 %copy.13 = f32[256,1024]{1,0:T(8,128)} copy(f32[256,1024]{1,0:T(8,128)S(1)} %get-tuple-element.6) | data formatting | bytes 2097152
  59.4 0.7 %copy.14 = f32[256,128]{1,0:T(8,128)} copy(f32[256,128]{1,0:T(8,128)S(1)} %get-tuple-element.7) | data formatting | bytes 262144
  60.0 0.7 %copy.15 = f32[256,128]{1,0:T(8,128)} copy(f32[256,128]{1,0:T(8,128)S(1)} %get-tuple-element.8) | data formatting | bytes 262144
Async XLA Ops:
  0.6 1.0 %copy-start = (bf16[256,1024]{1,0:T(8,128)(2,1)S(1)}, bf16[256,1024]{1,0:T(8,128)(2,1)}, u32[]{:S(2)}) copy-start(bf16[256,1024]{1,0:T(8,128)(2,1)} %q_hbm.1) | copy-start | bytes 1572868
  1.7 1.0 %copy-start.1 = (bf16[256,1024]{1,0:T(8,128)(2,1)S(1)}, bf16[256,1024]{1,0:T(8,128)(2,1)}, u32[]{:S(2)}) copy-start(bf16[256,1024]{1,0:T(8,128)(2,1)} %o_hbm.1) | copy-start | bytes 1572868
  2.7 1.0 %copy-start.2 = (bf16[256,1024]{1,0:T(8,128)(2,1)S(1)}, bf16[256,1024]{1,0:T(8,128)(2,1)}, u32[]{:S(2)}) copy-start(bf16[256,1024]{1,0:T(8,128)(2,1)} %g_hbm.1) | copy-start | bytes 1572868
  3.8 0.8 %copy-start.3 = (bf16[256,128]{1,0:T(8,128)(2,1)S(1)}, bf16[256,128]{1,0:T(8,128)(2,1)}, u32[]{:S(2)}) copy-start(bf16[256,128]{1,0:T(8,128)(2,1)} %k_hbm.1) | copy-start | bytes 196612
  4.6 0.8 %copy-start.4 = (bf16[256,128]{1,0:T(8,128)(2,1)S(1)}, bf16[256,128]{1,0:T(8,128)(2,1)}, u32[]{:S(2)}) copy-start(bf16[256,128]{1,0:T(8,128)(2,1)} %v_hbm.1) | copy-start | bytes 196612
  5.4 0.7 %copy-start.5 = (f32[8,256]{1,0:T(8,128)S(1)}, f32[8,256]{1,0:T(8,128)}, u32[]{:S(2)}) copy-start(f32[8,256]{1,0:T(8,128)} %lse_hbm.1) | copy-start | bytes 24580
  6.1 0.7 %copy-start.6 = (s32[2,512]{1,0:T(2,128)S(1)}, s32[2,512]{1,0:T(2,128)}, u32[]{:S(2)}) copy-start(s32[2,512]{1,0:T(2,128)} %spans.1) | copy-start | bytes 12292

commit v2 on v1

v2 whole, which is shorter than its diff:
```python
import functools
import math

import jax
import jax.numpy as jnp
from jax import lax
from jax.experimental import pallas as pl
from jax.experimental.pallas import tpu as pltpu
from jax.sharding import PartitionSpec as P

MESH = pl.DeviceIdType.MESH
HALF = 128
DIM = 128
HEADS = 8
WIDE = HEADS * HALF
NT = (((1,), (1,)), ((), ()))
NN = (((1,), (0,)), ((), ()))
TN = (((0,), (0,)), ((), ()))
LOG2E = math.log2(math.e)
SCALE = DIM ** (-0.5)

OWN, ONE, TWO, THREE, FOUR, OUTER = range(6)


def dot(a, b, dims):
    return lax.dot_general(a, b, dims, preferred_element_type=jnp.float32)


def less(a, b, shape):
    return jnp.full(shape, a, jnp.int32) < jnp.full(shape, b, jnp.int32)


def narrow(mask):
    return jnp.where(mask, 1.0, 0.0).astype(jnp.bfloat16) > 0.5


def ordered(swapped, first, second):
    return jnp.where(swapped, second, first), jnp.where(swapped, first, second)


def kernel(
    n_outer,
    n_inner,
    spans,
    q_hbm,
    k_hbm,
    v_hbm,
    o_hbm,
    g_hbm,
    lse_hbm,
    dq_out,
    dk_out,
    dv_out,
    q_in,
    o_in,
    g_in,
    lse_in,
    qn,
    gn,
    rows,
    kv,
    dq,
    own_acc,
    gout,
    gin,
    load_sem,
    kv_send,
    kv_recv,
    g_send,
    g_recv,
):
    outer = lax.axis_index("outer")
    inner = lax.axis_index("inner")
    core = lax.rem(inner, 2)

    def at(do, di):
        return (lax.rem(outer + do + n_outer, n_outer), lax.rem(inner + di + n_inner, n_inner))

    partner = (outer, inner + 1 - 2 * core)
    friends = [at(0, 2), at(0, -2), at(0, 4), at(0, -4), at(1, 0), at(-1, 0), partner]

    barrier = pltpu.get_barrier_semaphore()
    for friend in friends:
        pl.semaphore_signal(barrier, inc=1, device_id=friend, device_id_type=MESH)

    loads = [
        pltpu.make_async_copy(src, dst, load_sem.at[n])
        for n, (src, dst) in enumerate(
            [
                (g_hbm, g_in),
                (o_hbm, o_in),
                (q_hbm, q_in),
                (lse_hbm, lse_in),
                (k_hbm, kv.at[OWN, 0]),
                (v_hbm, kv.at[OWN, 1]),
            ]
        )
    ]
    for copy in loads:
        copy.start()

    def low_span(block):
        return jnp.minimum(spans[0, block], spans[1, block])

    def is_swapped(block, shape):
        return less(spans[1, block], spans[0, block], shape)

    own_block = outer * n_inner + inner
    own_low = low_span(own_block)
    swapped = is_swapped(own_block, (HALF, DIM))
    swapped_low = narrow(swapped)

    def kv_copies(sources, slot, number, target):
        return [
            pltpu.make_async_remote_copy(
                src_ref=sources[part],
                dst_ref=kv.at[slot, part],
                send_sem=kv_send.at[number, part],
                recv_sem=kv_recv.at[slot, part],
                device_id=target,
                device_id_type=MESH,
            )
            for part in range(2)
        ]

    args = [k_hbm, v_hbm]
    to_four = kv_copies(args, FOUR, 0, at(0, 4))
    to_two = kv_copies(args, TWO, 1, at(0, 2))
    to_outer = kv_copies(args, OUTER, 2, at(1, 0))
    even_one = kv_copies(args, ONE, 3, partner)
    even_three = kv_copies([kv.at[TWO, p] for p in range(2)], THREE, 4, partner)
    odd_one = kv_copies([kv.at[TWO, p] for p in range(2)], ONE, 3, partner)
    odd_three = kv_copies([kv.at[FOUR, p] for p in range(2)], THREE, 4, partner)

    def start(copies):
        for copy in copies:
            copy.start()

    def received(slot):
        for part in range(2):
            pltpu.make_async_remote_copy(
                src_ref=kv.at[slot, part],
                dst_ref=kv.at[slot, part],
                send_sem=kv_send.at[0, part],
                recv_sem=kv_recv.at[slot, part],
                device_id=partner,
                device_id_type=MESH,
            ).wait_recv()

    pl.semaphore_wait(barrier, len(friends))
    start(to_four)

    @pl.when(core == 0)
    def _():
        start(even_one)

    start(to_two)
    start(to_outer)

    for copy in loads:
        copy.wait()
    ones = jnp.ones((8, DIM), jnp.bfloat16)
    for h in range(HEADS):
        col = pl.ds(h * DIM, DIM)
        row = pl.ds(h * HALF, HALF)

        def halves(ref):
            return ordered(swapped_low, ref[pl.ds(0, HALF), col], ref[pl.ds(HALF, HALF), col])

        norms = ordered(swapped[:1], lse_in[h : h + 1, :HALF], lse_in[h : h + 1, HALF:])
        for half, (q, g, o, norm) in enumerate(zip(halves(q_in), halves(g_in), halves(o_in), norms)):
            qn[half, row, :] = q
            gn[half, row, :] = g
            product = g.astype(jnp.float32) * o.astype(jnp.float32)
            top = product.astype(jnp.bfloat16)
            rest = product - top.astype(jnp.float32)
            middle = rest.astype(jnp.bfloat16)
            low = (rest - middle.astype(jnp.float32)).astype(jnp.bfloat16)
            delta = dot(ones, top, NT) + dot(ones, middle, NT) + dot(ones, low, NT)
            rows[half, 0:1, row] = delta[0:1, :]
            rows[half, 1:2, row] = norm * LOG2E

    def attend(keys, q, norm):
        return jnp.exp2(dot(keys, q, NT) * (SCALE * LOG2E) - norm)

    def score_grads(p, values, g, delta):
        return (p * (dot(values, g, NT) - delta)).astype(jnp.bfloat16)

    def halves_of(slot, part, mask):
        return ordered(mask, kv[slot, part, pl.ds(0, HALF), :], kv[slot, part, pl.ds(HALF, HALF), :])

    def own():
        key_at = lax.broadcasted_iota(jnp.int32, (HALF, WIDE), 0)
        query_at = lax.rem(lax.broadcasted_iota(jnp.int32, (HALF, WIDE), 1), HALF)
        seen = key_at <= query_at
        k_lo, k_hi = halves_of(OWN, 0, swapped_low)
        v_lo, v_hi = halves_of(OWN, 1, swapped_low)
        keys = jnp.concatenate([k_lo, k_hi], 0)
        values = jnp.concatenate([v_lo, v_hi], 0)
        p_lo = jnp.where(seen, attend(k_lo, qn[0], rows[0, 1:2, :]), 0.0)
        p_hi = attend(keys, qn[1], rows[1, 1:2, :])
        p_hi = jnp.concatenate([p_hi[:HALF], jnp.where(seen, p_hi[HALF:], 0.0)], 0)
        s_lo = score_grads(p_lo, v_lo, gn[0], rows[0, 0:1, :])
        s_hi = score_grads(p_hi, values, gn[1], rows[1, 0:1, :])
        for part, (lo, hi, other_side) in enumerate(
            [(s_lo, s_hi, qn), (p_lo.astype(jnp.bfloat16), p_hi.astype(jnp.bfloat16), gn)]
        ):
            total = dot(hi, other_side[1], NN)
            first = total[:HALF] + dot(lo, other_side[0], NN)
            own_acc[part, pl.ds(0, HALF), :], own_acc[part, pl.ds(HALF, HALF), :] = ordered(
                swapped, first, total[HALF:]
            )
        dq[:, pl.ds(0, DIM)] = dot(s_lo, k_lo, TN)
        dq[:, pl.ds(DIM, DIM)] = dot(s_hi, keys, TN)

    def other(slot, do, di):
        there = at(do, di)
        block = there[0] * n_inner + there[1]
        low = low_span(block)
        early = less(low, own_low, (HALF, DIM))
        early_low = narrow(less(low, own_low, (WIDE, DIM)))
        early_row = less(low, own_low, (1, WIDE))
        turned = is_swapped(block, (HALF, DIM))
        turned_low = narrow(turned)
        k1, k_hi = halves_of(slot, 0, turned_low)
        v1, v_hi = halves_of(slot, 1, turned_low)
        k2 = jnp.where(early_low[:HALF], k1, k_hi)
        v2 = jnp.where(early_low[:HALF], v1, v_hi)
        q1, g1 = qn[1], gn[1]
        q2 = jnp.where(early_low, qn[0], q1)
        g2 = jnp.where(early_low, gn[0], g1)
        norm1, delta1 = rows[1, 1:2, :], rows[1, 0:1, :]
        norm2 = jnp.where(early_row, rows[0, 1:2, :], norm1)
        delta2 = jnp.where(early_row, rows[0, 0:1, :], delta1)
        p1 = attend(k1, q1, norm1)
        p2 = attend(k2, q2, norm2)
        s1 = score_grads(p1, v1, g1, delta1)
        s2 = score_grads(p2, v2, g2, delta2)
        for part, (first, second) in enumerate(
            [
                (dot(s1, q1, NN), dot(s2, q2, NN)),
                (dot(p1.astype(jnp.bfloat16), g1, NN), dot(p2.astype(jnp.bfloat16), g2, NN)),
            ]
        ):
            lo = first + jnp.where(early, second, 0.0)
            hi = jnp.where(early, 0.0, second)
            for half, value in enumerate(ordered(turned, lo, hi)):
                gout[slot, part, pl.ds(half * HALF, HALF), :] = value.astype(jnp.bfloat16)
        zero = jnp.zeros_like(k1)
        wide = jnp.concatenate(
            [
                jnp.concatenate([zero, k1], 1),
                jnp.concatenate(
                    [
                        jnp.where(early_low[:HALF], k2, zero),
                        jnp.where(early_low[:HALF], zero, k2),
                    ],
                    1,
                ),
            ],
            0,
        )
        dq[...] += dot(jnp.concatenate([s1, s2], 0), wide, TN)

    def g_copy(slot, target):
        return pltpu.make_async_remote_copy(
            src_ref=gout.at[slot],
            dst_ref=gin.at[slot],
            send_sem=g_send.at[slot],
            recv_sem=g_recv.at[slot],
            device_id=target,
            device_id_type=MESH,
        )

    g_two = g_copy(TWO, at(0, -2))
    g_four = g_copy(FOUR, at(0, -4))
    g_outer = g_copy(OUTER, at(-1, 0))
    g_one = g_copy(ONE, partner)
    g_three = g_copy(THREE, partner)

    def add_to(slot, extra):
        gout[slot] = (gout[slot].astype(jnp.float32) + gin[extra].astype(jnp.float32)).astype(
            jnp.bfloat16
        )

    def pick(even, odd):
        return even + core * (odd - even)

    own()

    slot = pick(FOUR, ONE)
    received(slot)
    other(slot, 0, -slot)

    @pl.when(core == 0)
    def _():
        g_four.start()

    @pl.when(core == 1)
    def _():
        g_one.start()
        received(FOUR)
        start(odd_three)

    @pl.when(core == 0)
    def _():
        received(THREE)

    slot = pick(THREE, FOUR)
    other(slot, 0, -slot)

    @pl.when(core == 0)
    def _():
        g_three.start()

    received(TWO)

    @pl.when(core == 0)
    def _():
        start(even_three)

    @pl.when(core == 1)
    def _():
        start(odd_one)

    other(TWO, 0, -2)

    @pl.when(core == 1)
    def _():
        g_three.wait_recv()
        add_to(FOUR, THREE)
        g_four.start()

    slot = pick(ONE, THREE)
    received(slot)
    other(slot, 0, -slot)

    @pl.when(core == 0)
    def _():
        g_one.start()

    @pl.when(core == 1)
    def _():
        g_three.start()

    received(OUTER)
    other(OUTER, -1, 0)
    g_outer.start()
    g_one.wait_recv()

    @pl.when(core == 0)
    def _():
        g_three.wait_recv()
        add_to(TWO, THREE)

    @pl.when(core == 1)
    def _():
        add_to(TWO, ONE)

    g_two.start()

    for h in range(HEADS):
        row = pl.ds(h * HALF, HALF)
        col = pl.ds(h * DIM, DIM)
        first, second = ordered(swapped, dq[row, pl.ds(0, DIM)], dq[row, pl.ds(DIM, DIM)])
        dq_out[pl.ds(0, HALF), col] = first * SCALE
        dq_out[pl.ds(HALF, HALF), col] = second * SCALE

    @pl.when(core == 0)
    def _():
        for part in range(2):
            own_acc[part] += gin[ONE, part].astype(jnp.float32)

    g_four.wait_recv()
    g_outer.wait_recv()
    g_two.wait_recv()
    for part, (out, factor) in enumerate([(dk_out, SCALE), (dv_out, 1.0)]):
        total = own_acc[part]
        for slot in (FOUR, OUTER, TWO):
            total = total + gin[slot, part].astype(jnp.float32)
        out[...] = total * factor
    for copies in (to_four, to_two, to_outer, odd_one, odd_three):
        for copy in copies:
            copy.wait_send()
    for copy in (g_two, g_four, g_outer, g_one, g_three):
        copy.wait_send()


def write_out(*refs):
    sources, results, sem = refs[:3], refs[3:6], refs[6]
    copies = [
        pltpu.make_async_copy(src, dst, sem.at[n])
        for n, (src, dst) in enumerate(zip(sources, results))
    ]
    for copy in copies:
        copy.start()
    for copy in copies:
        copy.wait()


def local(n_outer, n_inner, queries, keys, values, outputs, out_grads, log_sum_exp, span_ids):
    block, dim = keys.shape
    width = queries.shape[1]
    heads = log_sum_exp.shape[0]
    bf16, f32 = jnp.bfloat16, jnp.float32
    in_hbm = pl.BlockSpec(memory_space=pltpu.HBM)
    in_vmem = pl.BlockSpec(memory_space=pltpu.VMEM)
    arrays = [
        pltpu.with_memory_space_constraint(a, pltpu.HBM)
        for a in (queries, keys, values, outputs, out_grads, log_sum_exp)
    ]
    shapes = [(block, width), (block, dim), (block, dim)]
    grads = pl.pallas_call(
        functools.partial(kernel, n_outer, n_inner),
        out_shape=tuple(pltpu.VMEM(shape, f32) for shape in shapes),
        in_specs=[pl.BlockSpec(memory_space=pltpu.SMEM)] + [in_hbm] * 6,
        out_specs=(in_vmem,) * 3,
        scratch_shapes=[
            pltpu.VMEM((block, width), bf16),
            pltpu.VMEM((block, width), bf16),
            pltpu.VMEM((block, width), bf16),
            pltpu.VMEM((heads, block), f32),
            pltpu.VMEM((2, heads * HALF, dim), bf16),
            pltpu.VMEM((2, heads * HALF, dim), bf16),
            pltpu.VMEM((2, 8, heads * HALF), f32),
            pltpu.VMEM((6, 2, block, dim), bf16),
            pltpu.VMEM((heads * HALF, 2 * dim), f32),
            pltpu.VMEM((2, block, dim), f32),
            pltpu.VMEM((6, 2, block, dim), bf16),
            pltpu.VMEM((6, 2, block, dim), bf16),
            pltpu.SemaphoreType.DMA((6,)),
            pltpu.SemaphoreType.DMA((5, 2)),
            pltpu.SemaphoreType.DMA((6, 2)),
            pltpu.SemaphoreType.DMA((6,)),
            pltpu.SemaphoreType.DMA((6,)),
        ],
        compiler_params=pltpu.CompilerParams(
            collective_id=0, has_side_effects=True, vmem_limit_bytes=48 * 1024 * 1024
        ),
        name="backward",
    )(pltpu.with_memory_space_constraint(span_ids, pltpu.HBM), *arrays)
    return pl.pallas_call(
        write_out,
        out_shape=tuple(jax.ShapeDtypeStruct(shape, f32) for shape in shapes),
        in_specs=[in_vmem] * 3,
        out_specs=(pl.BlockSpec(memory_space=pl.ANY),) * 3,
        scratch_shapes=[pltpu.SemaphoreType.DMA((3,))],
        name="write_out",
    )(*(pltpu.with_memory_space_constraint(a, pltpu.VMEM) for a in grads))


def solution(mesh):
    tokens = P(("outer", "inner"), None)
    return jax.shard_map(
        functools.partial(local, mesh.shape["outer"], mesh.shape["inner"]),
        mesh=mesh,
        in_specs=(tokens,) * 5 + (P(None, ("outer", "inner")), P()),
        out_specs=(tokens,) * 3,
        check_vma=False,
    )
```

time: 61.1 us -> 40 us (0.65)
  the two profiles are of different devices: /device:TPU:14 before, /device:TPU:201 now
where the time goes in v2:
time: 40 us; the launch traced here: 39.9 us
  Pallas kernels  39.2 us (98%)
  between operations  0.64 us (2%)
    pallas_call x1, Pallas kernels, local(): pl.pallas_call(functools.partial(kernel, n_outer, n_inner), out_shape=tup...  38.1 us
    pallas_call x1, Pallas kernels, local(): pl.pallas_call(write_out, out_shape=tuple((jax.ShapeDtypeStruct(shape, f3...  1.07 us

profile of v2, /device:TPU:201, one launch (start us, length us, event | category | flops | bytes accessed | tf_op | source)
XLA Modules:
  0.0 39.9 jit_solution(6530870833286317165)
XLA Ops:
  0.6 38.1 %backward.1 = (f32[256,1024]{1,0:T(8,128)S(1)}, f32[256,128]{1,0:T(8,128)S(1)}, f32[256,128]{1,0:T(8,128)S(1)}) custom-call(s32[2,512]{1,0:T(2,128)} %spans.1, bf16[256,1024]{1,0:T(8,128)(2,1)} %q_hbm.1, bf16[256,128]{1,0:T(8,128)(2,1)} %k_hbm.1, bf16[256,128]{1,0:T(8,128)(2,1)} %v_hbm.1, bf16[256,1024]{1,0:T(8,128)(2,1)} %o_hbm.1, bf16[256,1024]{1,0:T(8,128)(2,1)} %g_hbm.1, ...), custom_call_target="tpu_custom_call" | custom-call | tf_op jit(solution)/shard_map/backward/pallas_call | solution.py:413
  38.8 1.1 %write_out.1 = (f32[256,1024]{1,0:T(8,128)}, f32[256,128]{1,0:T(8,128)}, f32[256,128]{1,0:T(8,128)}) custom-call(f32[256,1024]{1,0:T(8,128)S(1)} %get-tuple-element.6.refs_0_, f32[256,128]{1,0:T(8,128)S(1)} %get-tuple-element.7.refs_1_, f32[256,128]{1,0:T(8,128)S(1)} %get-tuple-element.8.refs_2_), custom_call_target="tpu_custom_call" | custom-call | tf_op jit(solution)/shard_map/write_out/pallas_call | solution.py:442

commit v3 on v2

--- a/solution.py
+++ b/solution.py
@@ -61,6 +61,7 @@
     kv,
     dq,
     own_acc,
+    weights,
     gout,
     gin,
     load_sem,
@@ -72,16 +73,17 @@
     outer = lax.axis_index("outer")
     inner = lax.axis_index("inner")
     core = lax.rem(inner, 2)
+    odd_outer = lax.rem(outer, 2)
 
     def at(do, di):
         return (lax.rem(outer + do + n_outer, n_outer), lax.rem(inner + di + n_inner, n_inner))
 
     partner = (outer, inner + 1 - 2 * core)
-    friends = [at(0, 2), at(0, -2), at(0, 4), at(0, -4), at(1, 0), at(-1, 0), partner]
+    senders = [at(0, -2), at(0, -4), at(-1, 0), partner]
 
     barrier = pltpu.get_barrier_semaphore()
-    for friend in friends:
-        pl.semaphore_signal(barrier, inc=1, device_id=friend, device_id_type=MESH)
+    for sender in senders:
+        pl.semaphore_signal(barrier, inc=1, device_id=sender, device_id_type=MESH)
 
     loads = [
         pltpu.make_async_copy(src, dst, load_sem.at[n])
@@ -125,6 +127,7 @@
 
     args = [k_hbm, v_hbm]
     to_four = kv_copies(args, FOUR, 0, at(0, 4))
+    on_four = kv_copies([kv.at[TWO, p] for p in range(2)], FOUR, 0, at(0, 2))
     to_two = kv_copies(args, TWO, 1, at(0, 2))
     to_outer = kv_copies(args, OUTER, 2, at(1, 0))
     even_one = kv_copies(args, ONE, 3, partner)
@@ -132,30 +135,30 @@
     odd_one = kv_copies([kv.at[TWO, p] for p in range(2)], ONE, 3, partner)
     odd_three = kv_copies([kv.at[FOUR, p] for p in range(2)], THREE, 4, partner)
 
-    def start(copies):
-        for copy in copies:
-            copy.start()
-
-    def received(slot):
-        for part in range(2):
-            pltpu.make_async_remote_copy(
-                src_ref=kv.at[slot, part],
-                dst_ref=kv.at[slot, part],
-                send_sem=kv_send.at[0, part],
-                recv_sem=kv_recv.at[slot, part],
-                device_id=partner,
-                device_id_type=MESH,
-            ).wait_recv()
-
-    pl.semaphore_wait(barrier, len(friends))
-    start(to_four)
-
-    @pl.when(core == 0)
-    def _():
-        start(even_one)
-
-    start(to_two)
-    start(to_outer)
+    def received(slot, part):
+        pltpu.make_async_remote_copy(
+            src_ref=kv.at[slot, part],
+            dst_ref=kv.at[slot, part],
+            send_sem=kv_send.at[0, part],
+            recv_sem=kv_recv.at[slot, part],
+            device_id=partner,
+            device_id_type=MESH,
+        ).wait_recv()
+
+    pl.semaphore_wait(barrier, len(senders))
+    for part in range(2):
+        to_two[part].start()
+
+        @pl.when(core == 0)
+        def _():
+            even_one[part].start()
+
+        @pl.when(odd_outer == 1)
+        def _():
+            to_four[part].start()
+
+    for part in range(2):
+        to_outer[part].start()
 
     for copy in loads:
         copy.wait()
@@ -213,39 +216,54 @@
         dq[:, pl.ds(0, DIM)] = dot(s_lo, k_lo, TN)
         dq[:, pl.ds(DIM, DIM)] = dot(s_hi, keys, TN)
 
-    def other(slot, do, di):
+    def sides(do, di):
         there = at(do, di)
         block = there[0] * n_inner + there[1]
         low = low_span(block)
-        early = less(low, own_low, (HALF, DIM))
-        early_low = narrow(less(low, own_low, (WIDE, DIM)))
-        early_row = less(low, own_low, (1, WIDE))
-        turned = is_swapped(block, (HALF, DIM))
-        turned_low = narrow(turned)
-        k1, k_hi = halves_of(slot, 0, turned_low)
-        v1, v_hi = halves_of(slot, 1, turned_low)
+        return (
+            less(low, own_low, (HALF, DIM)),
+            narrow(less(low, own_low, (WIDE, DIM))),
+            less(low, own_low, (1, WIDE)),
+            is_swapped(block, (HALF, DIM)),
+        )
+
+    def chosen(mask, ref, which):
+        other_half = ref[1, which, :] if which is not None else ref[1]
+        return jnp.where(mask, ref[0, which, :] if which is not None else ref[0], other_half)
+
+    def put(slot, part, first, second, early, turned):
+        lo = first + jnp.where(early, second, 0.0)
+        hi = jnp.where(early, 0.0, second)
+        for half, value in enumerate(ordered(turned, lo, hi)):
+            gout[slot, part, pl.ds(half * HALF, HALF), :] = value.astype(jnp.bfloat16)
+
+    def with_keys(slot, do, di, store):
+        early, early_low, early_row, turned = sides(do, di)
+        k1, k_hi = halves_of(slot, 0, narrow(turned))
+        k2 = jnp.where(early_low[:HALF], k1, k_hi)
+        q2 = chosen(early_low, qn, None)
+        g2 = chosen(early_low, gn, None)
+        norm2 = chosen(early_row, rows, pl.ds(1, 1))
+        p1 = attend(k1, qn[1], rows[1, 1:2, :])
+        p2 = attend(k2, q2, norm2)
+        weights[store, 0] = p1
+        weights[store, 1] = p2
+        first = dot(p1.astype(jnp.bfloat16), gn[1], NN)
+        second = dot(p2.astype(jnp.bfloat16), g2, NN)
+        put(slot, 1, first, second, early, turned)
+
+    def with_values(slot, do, di, store):
+        early, early_low, early_row, turned = sides(do, di)
+        k1, k_hi = halves_of(slot, 0, narrow(turned))
+        v1, v_hi = halves_of(slot, 1, narrow(turned))
         k2 = jnp.where(early_low[:HALF], k1, k_hi)
         v2 = jnp.where(early_low[:HALF], v1, v_hi)
-        q1, g1 = qn[1], gn[1]
-        q2 = jnp.where(early_low, qn[0], q1)
-        g2 = jnp.where(early_low, gn[0], g1)
-        norm1, delta1 = rows[1, 1:2, :], rows[1, 0:1, :]
-        norm2 = jnp.where(early_row, rows[0, 1:2, :], norm1)
-        delta2 = jnp.where(early_row, rows[0, 0:1, :], delta1)
-        p1 = attend(k1, q1, norm1)
-        p2 = attend(k2, q2, norm2)
-        s1 = score_grads(p1, v1, g1, delta1)
-        s2 = score_grads(p2, v2, g2, delta2)
-        for part, (first, second) in enumerate(
-            [
-                (dot(s1, q1, NN), dot(s2, q2, NN)),
-                (dot(p1.astype(jnp.bfloat16), g1, NN), dot(p2.astype(jnp.bfloat16), g2, NN)),
-            ]
-        ):
-            lo = first + jnp.where(early, second, 0.0)
-            hi = jnp.where(early, 0.0, second)
-            for half, value in enumerate(ordered(turned, lo, hi)):
-                gout[slot, part, pl.ds(half * HALF, HALF), :] = value.astype(jnp.bfloat16)
+        q2 = chosen(early_low, qn, None)
+        g2 = chosen(early_low, gn, None)
+        delta2 = chosen(early_row, rows, pl.ds(0, 1))
+        s1 = score_grads(weights[store, 0], v1, gn[1], rows[1, 0:1, :])
+        s2 = score_grads(weights[store, 1], v2, g2, delta2)
+        put(slot, 0, dot(s1, qn[1], NN), dot(s2, q2, NN), early, turned)
         zero = jnp.zeros_like(k1)
         wide = jnp.concatenate(
             [
@@ -262,102 +280,175 @@
         )
         dq[...] += dot(jnp.concatenate([s1, s2], 0), wide, TN)
 
-    def g_copy(slot, target):
-        return pltpu.make_async_remote_copy(
-            src_ref=gout.at[slot],
-            dst_ref=gin.at[slot],
-            send_sem=g_send.at[slot],
-            recv_sem=g_recv.at[slot],
-            device_id=target,
-            device_id_type=MESH,
-        )
-
-    g_two = g_copy(TWO, at(0, -2))
-    g_four = g_copy(FOUR, at(0, -4))
-    g_outer = g_copy(OUTER, at(-1, 0))
-    g_one = g_copy(ONE, partner)
-    g_three = g_copy(THREE, partner)
-
-    def add_to(slot, extra):
-        gout[slot] = (gout[slot].astype(jnp.float32) + gin[extra].astype(jnp.float32)).astype(
-            jnp.bfloat16
-        )
+    def g_copies(slot, target):
+        return [
+            pltpu.make_async_remote_copy(
+                src_ref=gout.at[slot, part],
+                dst_ref=gin.at[slot, part],
+                send_sem=g_send.at[slot, part],
+                recv_sem=g_recv.at[slot, part],
+                device_id=target,
+                device_id_type=MESH,
+            )
+            for part in range(2)
+        ]
+
+    g_two = g_copies(TWO, at(0, -2))
+    g_four = g_copies(FOUR, at(0, -4))
+    g_outer = g_copies(OUTER, at(-1, 0))
+    g_one = g_copies(ONE, partner)
+    g_three = g_copies(THREE, partner)
+
+    def add_to(slot, extra, part):
+        gout[slot, part] = (
+            gout[slot, part].astype(jnp.float32) + gin[extra, part].astype(jnp.float32)
+        ).astype(jnp.bfloat16)
 
     def pick(even, odd):
         return even + core * (odd - even)
 
+    def pass_on(part):
+        received(TWO, part)
+
+        @pl.when(odd_outer == 0)
+        def _():
+            on_four[part].start()
+
+        @pl.when(core == 0)
+        def _():
+            even_three[part].start()
+
+        @pl.when(core == 1)
+        def _():
+            odd_one[part].start()
+
+    K, V = 0, 1
     own()
 
-    slot = pick(FOUR, ONE)
-    received(slot)
-    other(slot, 0, -slot)
-
-    @pl.when(core == 0)
-    def _():
-        g_four.start()
-
-    @pl.when(core == 1)
-    def _():
-        g_one.start()
-        received(FOUR)
-        start(odd_three)
-
-    @pl.when(core == 0)
-    def _():
-        received(THREE)
-
-    slot = pick(THREE, FOUR)
-    other(slot, 0, -slot)
-
-    @pl.when(core == 0)
-    def _():
-        g_three.start()
-
-    received(TWO)
-
-    @pl.when(core == 0)
-    def _():
-        start(even_three)
-
-    @pl.when(core == 1)
-    def _():
-        start(odd_one)
-
-    other(TWO, 0, -2)
-
-    @pl.when(core == 1)
-    def _():
-        g_three.wait_recv()
-        add_to(FOUR, THREE)
-        g_four.start()
-
-    slot = pick(ONE, THREE)
-    received(slot)
-    other(slot, 0, -slot)
-
-    @pl.when(core == 0)
-    def _():
-        g_one.start()
-
-    @pl.when(core == 1)
-    def _():
-        g_three.start()
-
-    received(OUTER)
-    other(OUTER, -1, 0)
-    g_outer.start()
-    g_one.wait_recv()
-
-    @pl.when(core == 0)
-    def _():
-        g_three.wait_recv()
-        add_to(TWO, THREE)
-
-    @pl.when(core == 1)
-    def _():
-        add_to(TWO, ONE)
-
-    g_two.start()
+    @pl.when(core == 0)
+    def _():
+        pass_on(K)
+
+    @pl.when(core == 1)
+    def _():
+        received(ONE, K)
+
+    slot_a, slot_b = pick(TWO, ONE), pick(ONE, TWO)
+    with_keys(slot_a, 0, -slot_a, 0)
+
+    @pl.when(core == 0)
+    def _():
+        received(ONE, K)
+
+    @pl.when(core == 1)
+    def _():
+        g_one[V].start()
+        pass_on(K)
+
+    with_keys(slot_b, 0, -slot_b, 1)
+
+    @pl.when(core == 0)
+    def _():
+        g_one[V].start()
+
+    @pl.when(core == 1)
+    def _():
+        received(ONE, V)
+
+    pass_on(V)
+    with_values(slot_a, 0, -slot_a, 0)
+
+    @pl.when(core == 0)
+    def _():
+        received(ONE, V)
+
+    @pl.when(core == 1)
+    def _():
+        g_one[K].start()
+
+    with_values(slot_b, 0, -slot_b, 1)
+
+    @pl.when(core == 0)
+    def _():
+        g_one[K].start()
+
+    @pl.when(core == 1)
+    def _():
+        g_one[V].wait_recv()
+        add_to(TWO, ONE, V)
+        g_two[V].start()
+
+    slot_c, slot_d = pick(FOUR, THREE), pick(THREE, FOUR)
+    received(slot_c, K)
+    with_keys(slot_c, 0, -slot_c, 0)
+
+    @pl.when(core == 0)
+    def _():
+        g_four[V].start()
+        received(THREE, K)
+
+    @pl.when(core == 1)
+    def _():
+        g_three[V].start()
+        received(FOUR, K)
+        odd_three[K].start()
+
+    with_keys(slot_d, 0, -slot_d, 1)
+
+    @pl.when(core == 0)
+    def _():
+        g_three[V].start()
+        g_three[V].wait_recv()
+        add_to(TWO, THREE, V)
+        g_two[V].start()
+
+    @pl.when(core == 1)
+    def _():
+        g_one[K].wait_recv()
+        add_to(TWO, ONE, K)
+        g_two[K].start()
+
+    received(slot_c, V)
+    with_values(slot_c, 0, -slot_c, 0)
+
+    @pl.when(core == 0)
+    def _():
+        g_four[K].start()
+        received(THREE, V)
+
+    @pl.when(core == 1)
+    def _():
+        g_three[K].start()
+        received(FOUR, V)
+        odd_three[V].start()
+
+    with_values(slot_d, 0, -slot_d, 1)
+
+    @pl.when(core == 0)
+    def _():
+        g_three[K].start()
+        g_three[K].wait_recv()
+        add_to(TWO, THREE, K)
+        g_two[K].start()
+
+    @pl.when(core == 1)
+    def _():
+        g_three[V].wait_recv()
+        add_to(FOUR, THREE, V)
+        g_four[V].start()
+
+    received(OUTER, K)
+    with_keys(OUTER, -1, 0, 0)
+    g_outer[V].start()
+    received(OUTER, V)
+    with_values(OUTER, -1, 0, 0)
+    g_outer[K].start()
+
+    @pl.when(core == 1)
+    def _():
+        g_three[K].wait_recv()
+        add_to(FOUR, THREE, K)
+        g_four[K].start()
 
     for h in range(HEADS):
         row = pl.ds(h * HALF, HALF)
@@ -369,21 +460,21 @@
     @pl.when(core == 0)
     def _():
         for part in range(2):
+            g_one[part].wait_recv()
             own_acc[part] += gin[ONE, part].astype(jnp.float32)
 
-    g_four.wait_recv()
-    g_outer.wait_recv()
-    g_two.wait_recv()
-    for part, (out, factor) in enumerate([(dk_out, SCALE), (dv_out, 1.0)]):
+    for part, out, factor in [(V, dv_out, 1.0), (K, dk_out, SCALE)]:
         total = own_acc[part]
-        for slot in (FOUR, OUTER, TWO):
+        for slot, copies in [(TWO, g_two), (OUTER, g_outer), (FOUR, g_four)]:
+            copies[part].wait_recv()
             total = total + gin[slot, part].astype(jnp.float32)
         out[...] = total * factor
     for copies in (to_four, to_two, to_outer, odd_one, odd_three):
         for copy in copies:
             copy.wait_send()
-    for copy in (g_two, g_four, g_outer, g_one, g_three):
-        copy.wait_send()
+    for copies in (g_two, g_four, g_outer, g_one, g_three):
+        for copy in copies:
+            copy.wait_send()
 
 
 def write_out(*refs):
@@ -426,13 +517,14 @@
             pltpu.VMEM((6, 2, block, dim), bf16),
             pltpu.VMEM((heads * HALF, 2 * dim), f32),
             pltpu.VMEM((2, block, dim), f32),
+            pltpu.VMEM((2, 2, HALF, heads * HALF), f32),
             pltpu.VMEM((6, 2, block, dim), bf16),
             pltpu.VMEM((6, 2, block, dim), bf16),
             pltpu.SemaphoreType.DMA((6,)),
             pltpu.SemaphoreType.DMA((5, 2)),
             pltpu.SemaphoreType.DMA((6, 2)),
-            pltpu.SemaphoreType.DMA((6,)),
-            pltpu.SemaphoreType.DMA((6,)),
+            pltpu.SemaphoreType.DMA((6, 2)),
+            pltpu.SemaphoreType.DMA((6, 2)),
         ],
         compiler_params=pltpu.CompilerParams(
             collective_id=0, has_side_effects=True, vmem_limit_bytes=48 * 1024 * 1024

time: 40 us -> 36.4 us (0.910)
  the two profiles are of different devices: /device:TPU:201 before, /device:TPU:1 now
where the time goes in v3:
time: 36.4 us; the launch traced here: 36.2 us
  Pallas kernels  35.6 us (98%)
  between operations  0.64 us (2%)
    pallas_call x1, Pallas kernels, local(): pl.pallas_call(functools.partial(kernel, n_outer, n_inner), out_shape=tup...  34.5 us
    pallas_call x1, Pallas kernels, local(): pl.pallas_call(write_out, out_shape=tuple((jax.ShapeDtypeStruct(shape, f3...  1.07 us

profile of v3, /device:TPU:1, one launch (start us, length us, event | category | flops | bytes accessed | tf_op | source)
XLA Modules:
  0.0 36.2 jit_solution(11484382430214539619)
XLA Ops:
  0.6 34.5 %backward.1 = (f32[256,1024]{1,0:T(8,128)S(1)}, f32[256,128]{1,0:T(8,128)S(1)}, f32[256,128]{1,0:T(8,128)S(1)}) custom-call(s32[2,512]{1,0:T(2,128)} %spans.1, bf16[256,1024]{1,0:T(8,128)(2,1)} %q_hbm.1, bf16[256,128]{1,0:T(8,128)(2,1)} %k_hbm.1, bf16[256,128]{1,0:T(8,128)(2,1)} %v_hbm.1, bf16[256,1024]{1,0:T(8,128)(2,1)} %o_hbm.1, bf16[256,1024]{1,0:T(8,128)(2,1)} %g_hbm.1, ...), custom_call_target="tpu_custom_call" | custom-call | tf_op jit(solution)/shard_map/backward/pallas_call | solution.py:504
  35.1 1.1 %write_out.1 = (f32[256,1024]{1,0:T(8,128)}, f32[256,128]{1,0:T(8,128)}, f32[256,128]{1,0:T(8,128)}) custom-call(f32[256,1024]{1,0:T(8,128)S(1)} %get-tuple-element.6.refs_0_, f32[256,128]{1,0:T(8,128)S(1)} %get-tuple-element.7.refs_1_, f32[256,128]{1,0:T(8,128)S(1)} %get-tuple-element.8.refs_2_), custom_call_target="tpu_custom_call" | custom-call | tf_op jit(solution)/shard_map/write_out/pallas_call | solution.py:534

commit v4 on v3

--- a/solution.py
+++ b/solution.py
@@ -41,7 +41,7 @@
 def kernel(
     n_outer,
     n_inner,
-    spans,
+    spans_hbm,
     q_hbm,
     k_hbm,
     v_hbm,
@@ -51,6 +51,7 @@
     dq_out,
     dk_out,
     dv_out,
+    spans,
     q_in,
     o_in,
     g_in,
@@ -95,6 +96,7 @@
                 (lse_hbm, lse_in),
                 (k_hbm, kv.at[OWN, 0]),
                 (v_hbm, kv.at[OWN, 1]),
+                (spans_hbm, spans),
             ]
         )
     ]
@@ -106,11 +108,6 @@
 
     def is_swapped(block, shape):
         return less(spans[1, block], spans[0, block], shape)
-
-    own_block = outer * n_inner + inner
-    own_low = low_span(own_block)
-    swapped = is_swapped(own_block, (HALF, DIM))
-    swapped_low = narrow(swapped)
 
     def kv_copies(sources, slot, number, target):
         return [
@@ -162,6 +159,10 @@
 
     for copy in loads:
         copy.wait()
+    own_block = outer * n_inner + inner
+    own_low = low_span(own_block)
+    swapped = is_swapped(own_block, (HALF, DIM))
+    swapped_low = narrow(swapped)
     ones = jnp.ones((8, DIM), jnp.bfloat16)
     for h in range(HEADS):
         col = pl.ds(h * DIM, DIM)
@@ -294,7 +295,7 @@
         ]
 
     g_two = g_copies(TWO, at(0, -2))
-    g_four = g_copies(FOUR, at(0, -4))
+    g_four = g_copies(FOUR, at(0, -4 + 2 * odd_outer))
     g_outer = g_copies(OUTER, at(-1, 0))
     g_one = g_copies(ONE, partner)
     g_three = g_copies(THREE, partner)
@@ -323,6 +324,18 @@
             odd_one[part].start()
 
     K, V = 0, 1
+
+    def merge(copies, slot, extra, arrived, part):
+        arrived[part].wait_recv()
+        add_to(slot, extra, part)
+        if copies is not None:
+            copies[part].start()
+
+    def send_two(part):
+        @pl.when(odd_outer == 0)
+        def _():
+            g_two[part].start()
+
     own()
 
     @pl.when(core == 0)
@@ -374,68 +387,48 @@
 
     @pl.when(core == 1)
     def _():
-        g_one[V].wait_recv()
-        add_to(TWO, ONE, V)
-        g_two[V].start()
-
-    slot_c, slot_d = pick(FOUR, THREE), pick(THREE, FOUR)
-    received(slot_c, K)
-    with_keys(slot_c, 0, -slot_c, 0)
-
-    @pl.when(core == 0)
-    def _():
+        received(THREE, K)
+        with_keys(THREE, 0, -THREE, 0)
+        g_three[V].start()
+        merge(None, TWO, ONE, g_one, V)
+        send_two(V)
+        received(THREE, V)
+        with_values(THREE, 0, -THREE, 0)
+        g_three[K].start()
+        merge(None, TWO, ONE, g_one, K)
+        send_two(K)
+
+
+    @pl.when(core == 0)
+    def _():
+        merge(None, TWO, THREE, g_three, V)
+        send_two(V)
+        merge(None, TWO, THREE, g_three, K)
+        send_two(K)
+
+        received(FOUR, K)
+        with_keys(FOUR, 0, -FOUR, 0)
         g_four[V].start()
         received(THREE, K)
+        with_keys(THREE, 0, -THREE, 1)
+        g_three[V].start()
+        received(FOUR, V)
+        with_values(FOUR, 0, -FOUR, 0)
+        g_four[K].start()
+        received(THREE, V)
+        with_values(THREE, 0, -THREE, 1)
+        g_three[K].start()
 
     @pl.when(core == 1)
     def _():
-        g_three[V].start()
         received(FOUR, K)
         odd_three[K].start()
-
-    with_keys(slot_d, 0, -slot_d, 1)
-
-    @pl.when(core == 0)
-    def _():
-        g_three[V].start()
-        g_three[V].wait_recv()
-        add_to(TWO, THREE, V)
-        g_two[V].start()
-
-    @pl.when(core == 1)
-    def _():
-        g_one[K].wait_recv()
-        add_to(TWO, ONE, K)
-        g_two[K].start()
-
-    received(slot_c, V)
-    with_values(slot_c, 0, -slot_c, 0)
-
-    @pl.when(core == 0)
-    def _():
-        g_four[K].start()
-        received(THREE, V)
-
-    @pl.when(core == 1)
-    def _():
-        g_three[K].start()
+        with_keys(FOUR, 0, -FOUR, 0)
         received(FOUR, V)
         odd_three[V].start()
-
-    with_values(slot_d, 0, -slot_d, 1)
-
-    @pl.when(core == 0)
-    def _():
-        g_three[K].start()
-        g_three[K].wait_recv()
-        add_to(TWO, THREE, K)
-        g_two[K].start()
-
-    @pl.when(core == 1)
-    def _():
-        g_three[V].wait_recv()
-        add_to(FOUR, THREE, V)
-        g_four[V].start()
+        with_values(FOUR, 0, -FOUR, 0)
+        merge(g_four, FOUR, THREE, g_three, V)
+        merge(g_four, FOUR, THREE, g_three, K)
 
     received(OUTER, K)
     with_keys(OUTER, -1, 0, 0)
@@ -444,11 +437,11 @@
     with_values(OUTER, -1, 0, 0)
     g_outer[K].start()
 
-    @pl.when(core == 1)
-    def _():
-        g_three[K].wait_recv()
-        add_to(FOUR, THREE, K)
-        g_four[K].start()
+
+    @pl.when(odd_outer == 1)
+    def _():
+        merge(g_two, TWO, FOUR, g_four, V)
+        merge(g_two, TWO, FOUR, g_four, K)
 
     for h in range(HEADS):
         row = pl.ds(h * HALF, HALF)
@@ -465,10 +458,17 @@
 
     for part, out, factor in [(V, dv_out, 1.0), (K, dk_out, SCALE)]:
         total = own_acc[part]
-        for slot, copies in [(TWO, g_two), (OUTER, g_outer), (FOUR, g_four)]:
+        for slot, copies in [(OUTER, g_outer), (TWO, g_two)]:
             copies[part].wait_recv()
             total = total + gin[slot, part].astype(jnp.float32)
-        out[...] = total * factor
+        own_acc[part] = total
+
+        @pl.when(odd_outer == 0)
+        def _():
+            g_four[part].wait_recv()
+            own_acc[part] += gin[FOUR, part].astype(jnp.float32)
+
+        out[...] = own_acc[part] * factor
     for copies in (to_four, to_two, to_outer, odd_one, odd_three):
         for copy in copies:
             copy.wait_send()
@@ -504,9 +504,10 @@
     grads = pl.pallas_call(
         functools.partial(kernel, n_outer, n_inner),
         out_shape=tuple(pltpu.VMEM(shape, f32) for shape in shapes),
-        in_specs=[pl.BlockSpec(memory_space=pltpu.SMEM)] + [in_hbm] * 6,
+        in_specs=[in_hbm] * 7,
         out_specs=(in_vmem,) * 3,
         scratch_shapes=[
+            pltpu.SMEM(span_ids.shape, jnp.int32),
             pltpu.VMEM((block, width), bf16),
             pltpu.VMEM((block, width), bf16),
             pltpu.VMEM((block, width), bf16),
@@ -520,7 +521,7 @@
             pltpu.VMEM((2, 2, HALF, heads * HALF), f32),
             pltpu.VMEM((6, 2, block, dim), bf16),
             pltpu.VMEM((6, 2, block, dim), bf16),
-            pltpu.SemaphoreType.DMA((6,)),
+            pltpu.SemaphoreType.DMA((7,)),
             pltpu.SemaphoreType.DMA((5, 2)),
             pltpu.SemaphoreType.DMA((6, 2)),
             pltpu.SemaphoreType.DMA((6, 2)),

time: 36.4 us -> 35.7 us (0.981)
  the two profiles are of different devices: /device:TPU:1 before, /device:TPU:201 now
where the time goes in v4:
time: 35.7 us; the launch traced here: 35.6 us
  Pallas kernels  34.9 us (98%)
  between operations  0.64 us (2%)
    pallas_call x1, Pallas kernels, local(): pl.pallas_call(functools.partial(kernel, n_outer, n_inner), out_shape=tup...  33.9 us
    pallas_call x1, Pallas kernels, local(): pl.pallas_call(write_out, out_shape=tuple((jax.ShapeDtypeStruct(shape, f3...  1.07 us

profile of v4, /device:TPU:201, one launch (start us, length us, event | category | flops | bytes accessed | tf_op | source)
XLA Modules:
  0.0 35.6 jit_solution(7826293663305693982)
XLA Ops:
  0.6 33.9 %backward.1 = (f32[256,1024]{1,0:T(8,128)S(1)}, f32[256,128]{1,0:T(8,128)S(1)}, f32[256,128]{1,0:T(8,128)S(1)}) custom-call(s32[2,512]{1,0:T(2,128)} %spans_hbm.1, bf16[256,1024]{1,0:T(8,128)(2,1)} %q_hbm.1, bf16[256,128]{1,0:T(8,128)(2,1)} %k_hbm.1, bf16[256,128]{1,0:T(8,128)(2,1)} %v_hbm.1, bf16[256,1024]{1,0:T(8,128)(2,1)} %o_hbm.1, ...), custom_call_target="tpu_custom_call" | custom-call | tf_op jit(solution)/shard_map/backward/pallas_call | solution.py:504
  34.5 1.1 %write_out.1 = (f32[256,1024]{1,0:T(8,128)}, f32[256,128]{1,0:T(8,128)}, f32[256,128]{1,0:T(8,128)}) custom-call(f32[256,1024]{1,0:T(8,128)S(1)} %get-tuple-element.6.refs_0_, f32[256,128]{1,0:T(8,128)S(1)} %get-tuple-element.7.refs_1_, f32[256,128]{1,0:T(8,128)S(1)} %get-tuple-element.8.refs_2_), custom_call_target="tpu_custom_call" | custom-call | tf_op jit(solution)/shard_map/write_out/pallas_call | solution.py:535

commit v5 on v4

--- a/solution.py
+++ b/solution.py
@@ -154,8 +154,10 @@
         def _():
             to_four[part].start()
 
-    for part in range(2):
-        to_outer[part].start()
+    @pl.when(odd_outer == 1)
+    def _():
+        for part in range(2):
+            to_outer[part].start()
 
     for copy in loads:
         copy.wait()
@@ -314,6 +316,9 @@
         @pl.when(odd_outer == 0)
         def _():
             on_four[part].start()
+            if part == 0:
+                to_outer[0].start()
+                to_outer[1].start()
 
         @pl.when(core == 0)
         def _():
@@ -433,15 +438,19 @@
     received(OUTER, K)
     with_keys(OUTER, -1, 0, 0)
     g_outer[V].start()
+
+    @pl.when(odd_outer == 1)
+    def _():
+        merge(g_two, TWO, FOUR, g_four, V)
+
     received(OUTER, V)
     with_values(OUTER, -1, 0, 0)
     g_outer[K].start()
 
-
     @pl.when(odd_outer == 1)
     def _():
-        merge(g_two, TWO, FOUR, g_four, V)
         merge(g_two, TWO, FOUR, g_four, K)
+
 
     for h in range(HEADS):
         row = pl.ds(h * HALF, HALF)

time: 35.7 us -> 34.8 us (0.975)
  the two profiles are of different devices: /device:TPU:201 before, /device:TPU:65 now
where the time goes in v5:
time: 34.8 us; the launch traced here: 34.7 us
  Pallas kernels  34.1 us (98%)
  between operations  0.64 us (2%)
    pallas_call x1, Pallas kernels, local(): pl.pallas_call(functools.partial(kernel, n_outer, n_inner), out_shape=tup...  33 us
    pallas_call x1, Pallas kernels, local(): pl.pallas_call(write_out, out_shape=tuple((jax.ShapeDtypeStruct(shape, f3...  1.07 us

profile of v5, /device:TPU:65, one launch (start us, length us, event | category | flops | bytes accessed | tf_op | source)
XLA Modules:
  0.0 34.7 jit_solution(12987174198067741566)
XLA Ops:
  0.6 33.0 %backward.1 = (f32[256,1024]{1,0:T(8,128)S(1)}, f32[256,128]{1,0:T(8,128)S(1)}, f32[256,128]{1,0:T(8,128)S(1)}) custom-call(s32[2,512]{1,0:T(2,128)} %spans_hbm.1, bf16[256,1024]{1,0:T(8,128)(2,1)} %q_hbm.1, bf16[256,128]{1,0:T(8,128)(2,1)} %k_hbm.1, bf16[256,128]{1,0:T(8,128)(2,1)} %v_hbm.1, bf16[256,1024]{1,0:T(8,128)(2,1)} %o_hbm.1, ...), custom_call_target="tpu_custom_call" | custom-call | tf_op jit(solution)/shard_map/backward/pallas_call | solution.py:513
  33.6 1.1 %write_out.1 = (f32[256,1024]{1,0:T(8,128)}, f32[256,128]{1,0:T(8,128)}, f32[256,128]{1,0:T(8,128)}) custom-call(f32[256,1024]{1,0:T(8,128)S(1)} %get-tuple-element.6.refs_0_, f32[256,128]{1,0:T(8,128)S(1)} %get-tuple-element.7.refs_1_, f32[256,128]{1,0:T(8,128)S(1)} %get-tuple-element.8.refs_2_), custom_call_target="tpu_custom_call" | custom-call | tf_op jit(solution)/shard_map/write_out/pallas_call | solution.py:544

commit v6 on v5

--- a/solution.py
+++ b/solution.py
@@ -417,12 +417,12 @@
         received(THREE, K)
         with_keys(THREE, 0, -THREE, 1)
         g_three[V].start()
+        received(THREE, V)
+        with_values(THREE, 0, -THREE, 1)
+        g_three[K].start()
         received(FOUR, V)
         with_values(FOUR, 0, -FOUR, 0)
         g_four[K].start()
-        received(THREE, V)
-        with_values(THREE, 0, -THREE, 1)
-        g_three[K].start()
 
     @pl.when(core == 1)
     def _():

time: 34.8 us -> 34.6 us (level)
  the two profiles are of different devices: /device:TPU:65 before, /device:TPU:127 now
where the time goes in v6:
time: 34.6 us; the launch traced here: 34.5 us
  Pallas kernels  33.8 us (98%)
  between operations  0.64 us (2%)
    pallas_call x1, Pallas kernels, local(): pl.pallas_call(functools.partial(kernel, n_outer, n_inner), out_shape=tup...  32.8 us
    pallas_call x1, Pallas kernels, local(): pl.pallas_call(write_out, out_shape=tuple((jax.ShapeDtypeStruct(shape, f3...  1.07 us

profile of v6, /device:TPU:127, one launch (start us, length us, event | category | flops | bytes accessed | tf_op | source)
XLA Modules:
  0.0 34.5 jit_solution(1469770463324443242)
XLA Ops:
  0.6 32.8 %backward.1 = (f32[256,1024]{1,0:T(8,128)S(1)}, f32[256,128]{1,0:T(8,128)S(1)}, f32[256,128]{1,0:T(8,128)S(1)}) custom-call(s32[2,512]{1,0:T(2,128)} %spans_hbm.1, bf16[256,1024]{1,0:T(8,128)(2,1)} %q_hbm.1, bf16[256,128]{1,0:T(8,128)(2,1)} %k_hbm.1, bf16[256,128]{1,0:T(8,128)(2,1)} %v_hbm.1, bf16[256,1024]{1,0:T(8,128)(2,1)} %o_hbm.1, ...), custom_call_target="tpu_custom_call" | custom-call | tf_op jit(solution)/shard_map/backward/pallas_call | solution.py:513
  33.4 1.1 %write_out.1 = (f32[256,1024]{1,0:T(8,128)}, f32[256,128]{1,0:T(8,128)}, f32[256,128]{1,0:T(8,128)}) custom-call(f32[256,1024]{1,0:T(8,128)S(1)} %get-tuple-element.6.refs_0_, f32[256,128]{1,0:T(8,128)S(1)} %get-tuple-element.7.refs_1_, f32[256,128]{1,0:T(8,128)S(1)} %get-tuple-element.8.refs_2_), custom_call_target="tpu_custom_call" | custom-call | tf_op jit(solution)/shard_map/write_out/pallas_call | solution.py:544
